TPU v7x, 32 devices: a whole 2x2x4 slice. The times are simulated.
32 devices in a mesh: gx: 4 (over z), gy: 4 (over x, core), gz: 2 (over y).
Axes of the slice: x: 2, y: 2, z: 4, core: 2. Of those that a mesh axis runs over, the one named last changes fastest.
Arguments:
- coarse_fields: float32 [4, 64, 64, 256], P(None, 'gx', 'gy', 'gz'), may hold values from -6 to 6
- coarse_wind: float32 [3, 64, 64, 256], P(None, 'gx', 'gy', 'gz'), may hold values from -0.4 to 0.4
- fine_fields: float32 [4, 128, 64, 256], P(None, 'gx', 'gy', 'gz'), may hold values from -6 to 6
- fine_wind: float32 [3, 128, 64, 256], P(None, 'gx', 'gy', 'gz'), may hold values from -0.4 to 0.4
- fine_owner: int32 [4, 4, 2], P('gx', 'gy', 'gz'), may hold values from 0 to 3, as said below
Outputs:
- coarse_next: float32 [4, 64, 64, 256], P(None, 'gx', 'gy', 'gz')
- fine_next: float32 [4, 128, 64, 256], P(None, 'gx', 'gy', 'gz')
Inputs may be any that keep to these rules, and one draw needn't show every extreme that they name: `fine_owner`: in each row of fine boxes along the first direction (fixed second and third index), fine box i refines coarse box (i + r) mod 4 for an offset r of that row, so every row names every coarse box once.
All inputs are finite; a program needn't handle non-finite values.
Results may differ from a plain program's by a relative error of at most 0.0003.
Values sent between devices are 32-bit elements; how exact they have to be, the bound alone decides.
No kernel may reach another device: no remote copies, remote signals or barrier semaphores. Data moves between devices by JAX's collectives and lax.ppermute only.
A program may use at most 128 MiB of HBM per device.

v0:
```python
import functools

import jax
import jax.numpy as jnp
from jax import lax
from jax.experimental import pallas as pl
from jax.experimental.pallas import tpu as pltpu
from jax.sharding import PartitionSpec as P

diffusion = 0.05
section_weights = (1.0 / 3.0, 0.5, 1.0)
F32 = jnp.float32
BF16 = jnp.bfloat16
PAD = 32
TOP = 8


class Sizes:
    def __init__(self, coarse_shape, fine_shape):
        self.q, self.x, self.y, self.z = coarse_shape
        self.fx = fine_shape[1]
        self.ly, self.sy = self.y // 4, self.y // 2
        self.lz, self.sz = self.z // 4, self.z // 2
        self.ex = self.x + 4
        self.ep = -(-self.ex // 8) * 8
        self.fe = self.fx + 4
        self.halo = 3 * self.q + 6
        self.rows_f, self.rows_w = self.q * (3 * self.x + 6), 3 * (2 * self.x + 2)
        self.rows_y = 3 * self.q * self.ex
        self.rows_e = self.rows_y + self.ep
        self.rows_z = self.sy + 2
        self.slab = self.rows_e + self.q * self.rows_z
        assert self.q == 4 and self.y == 16 and self.z == 128 and self.ex <= 20 and self.fx == 2 * self.x


def lanes_of(shape):
    return lax.broadcasted_iota(jnp.int32, shape, len(shape) - 1)


def halves(value):
    high = value.astype(BF16)
    return high, (value - high.astype(F32)).astype(BF16)


def times(value, matrix):
    high, low = halves(value)
    return jnp.dot(high, matrix, preferred_element_type=F32) + jnp.dot(low, matrix, preferred_element_type=F32)


def scaled(wind):
    return [w * (-0.5 / diffusion) for w in wind]


def advanced(base, fraction, wind, center, x_low, x_high, y_low, y_high, z_low, z_high):
    total = (x_high + x_low) + wind[0] * (x_high - x_low)
    total = total + ((y_high + y_low) + wind[1] * (y_high - y_low))
    total = total + ((z_high + z_low) + wind[2] * (z_high - z_low))
    if base is None:
        return center * (1.0 - 6.0 * diffusion * fraction) + total * (diffusion * fraction)
    return (base - center * (6.0 * diffusion * fraction)) + total * (diffusion * fraction)


def layer_of(s, own, low, high, member, at, width, first):
    size = own.shape[1]
    if at < 0:
        return low[first + width * member + at + width]
    if at >= size:
        return high[first + width * member + at - size]
    return own[member, at]


def unrolled(begin, end, at_once, body, carry=None):
    while (end - begin) % at_once:
        at_once -= 1

    def several(i, carry):
        for more in range(at_once):
            carry = body(begin + i * at_once + more, carry)
        return carry

    return lax.fori_loop(0, (end - begin) // at_once, several, carry)


def pack_kernel(s, fields, wind, up, down, sems):
    size = fields.shape[1]
    moves = []
    for own, members, width, first in ((fields, s.q, 3, 0), (wind, 3, 2, 3 * s.q)):
        for dst, at in ((up, size - width), (down, 0)):
            place = dst.at[first : first + members * width].reshape(members, width, s.y, s.z)
            moves.append((own.at[:, at : at + width], place))
    moves = [pltpu.make_async_copy(src, dst, sems.at[i]) for i, (src, dst) in enumerate(moves)]
    for move in moves:
        move.start()
    for move in moves:
        move.wait()


def y_rows(s, members, width):
    below, above = [], []
    for out, extra in ((below, lambda r: r), (above, lambda r: width - 1 - r)):
        at = 0
        for m in range(members):
            for r in range(width):
                out.append((m, r, extra(r), at))
                at += s.x + 2 * extra(r)
    return below, above


def ypack_kernel(s, c0, cw, lo, hi, up, dn):
    x, y, z = s.x, s.y, s.z
    flat_lo = lo.reshape(s.halo * y, z)
    flat_hi = hi.reshape(s.halo * y, z)
    for own, members, width, first, place in ((c0, s.q, 3, 0, 0), (cw, 3, 2, 3 * s.q, s.rows_f)):
        flat = own.reshape(members * x * y, z)
        for dst, rows, start in zip((up, dn), y_rows(s, members, width), (y - width, 0)):
            for m, r, e, at in rows:
                row, at = start + r, at + place
                if e:
                    dst[at : at + e, :] = flat_lo[pl.ds((first + width * (m + 1) - e) * y + row, e, stride=y), :]
                    dst[at + e + x : at + x + 2 * e, :] = flat_hi[pl.ds((first + width * m) * y + row, e, stride=y), :]
                dst[at + e : at + e + x, :] = flat[pl.ds(m * x * y + row, x, stride=y), :]


EDGE = 4


def turned(base, fraction, wind, center, x_low, x_high):
    y, z = center.shape
    return advanced(
        base,
        fraction,
        wind,
        center,
        x_low,
        x_high,
        pltpu.roll(center, 1, 0),
        pltpu.roll(center, y - 1, 0),
        pltpu.roll(center, 1, 1),
        pltpu.roll(center, z - 1, 1),
    )


def slab_parts(s, rows_of, tile_of, layers_of, put):
    q, y, z = s.q, s.y, s.z
    lane_y = lanes_of((y, z))
    columns = (lane_y == s.lz - 1) | (lane_y == s.lz) | (lane_y == s.lz + s.sz - 1) | (lane_y == s.lz + s.sz)
    low_at = (lane_y % 2 == 0) & (lane_y < z // 2)
    high_at = (lane_y % 2 == 0) & (lane_y >= z // 2)
    ends = None
    for f in range(q):
        zfaces = None
        for k in range(3):
            rows = [rows_of(k, f, row) for row in (s.ly - 1, s.ly, s.ly + s.sy - 1, s.ly + s.sy)]
            sides = (0.75 * rows[0] + 0.25 * rows[1], 0.25 * rows[2] + 0.75 * rows[3])
            lane_x = lanes_of(sides[0].shape)
            put(
                "y",
                (k * q + f) * s.ex,
                jnp.where(lane_x < s.sz, pltpu.roll(sides[0], z - s.lz, 1), pltpu.roll(sides[1], s.lz, 1)),
            )
            for side in range(2):
                e = 4 * (q * k + f) + 2 * side + 1
                before = jnp.where(lane_x == s.lz - 1, sides[side], 0.0)
                after = jnp.where(lane_x == s.lz + s.sz, sides[side], 0.0)
                part = pltpu.roll(before, (e - s.lz + 1) % z, 1) + pltpu.roll(after, (e - 1 - s.lz - s.sz) % z, 1)
                ends = part if ends is None else ends + part
            raw = None
            for a in layers_of(k):
                part = jnp.where(columns, tile_of(k, f, a), 0.0)
                part = pltpu.roll(part, (2 * a - s.lz + 1) % z, 1)
                raw = part if raw is None else raw + part
            beside = pltpu.roll(raw, z - 1, 1)
            low = jnp.where(low_at, 0.75 * raw + 0.25 * beside, 0.0)
            high = jnp.where(high_at, 0.25 * raw + 0.75 * beside, 0.0)
            part = pltpu.roll(low, (2 * s.ex * k - 1) % z, 1) + pltpu.roll(high, (2 * s.ex * k - z // 2) % z, 1)
            zfaces = part if zfaces is None else zfaces + part
        put("z", s.rows_e + f * s.rows_z, zfaces[s.ly - 1 : s.ly + s.sy + 1])
    put("e", s.rows_y, ends)


def inner_kernel(s, c0, cw, part, near, state1, state2):
    q, x, y, z = s.q, s.x, s.y, s.z
    states = (c0, state1, state2)
    for step in range(2):
        src, dst = states[step], states[step + 1]

        def layer(j, carry, step=step, src=src, dst=dst):
            w = scaled([cw[d, j] for d in range(3)])
            for f in range(q):
                base = None if step == 0 else c0[f, j]
                dst[f, j] = turned(base, section_weights[step], w, src[f, j], src[f, j - 1], src[f, j + 1])
            return carry

        unrolled(step + 1, x - 1 - step, 7 if step == 0 else 6, layer)
    for f in range(q):
        near[f, 0] = state1[f, EDGE - 2]
        near[f, 1] = state1[f, x + 1 - EDGE]
    count = s.ex - 2 * EDGE
    part[...] = jnp.zeros_like(part)

    def rows_of(k, f, row):
        flat = states[k].reshape(q * x * y, z)
        return flat[pl.ds((f * x + EDGE - 2) * y + row, count, stride=y), :]

    def put(kind, at, rows):
        if kind == "z":
            part[at : at + s.rows_z, :] = rows
        else:
            part[at + EDGE : at + EDGE + count, :] = rows

    slab_parts(s, rows_of, lambda k, f, a: states[k][f, a - 2], lambda k: range(EDGE, s.ex - EDGE), put)


def slab_kernel(s, c0, cw, lo, hi, part, near, slab, ends0, ends1, ends2):
    q, x, y, z = s.q, s.x, s.y, s.z
    states = (ends0, ends1, ends2)
    places = list(range(-2, EDGE - 2)) + list(range(x + 2 - EDGE, x + 2))
    slab[...] = part[...]
    for j, at in enumerate(places):
        for f in range(q):
            ends0[f, j] = layer_of(s, c0, lo, hi, f, at, 3, 0)
    for step in range(2):
        for j, at in enumerate(places):
            if step == 1 and at in (-2, x + 1):
                for f in range(q):
                    ends2[f, j] = jnp.zeros((y, z), F32)
                continue
            w = scaled([layer_of(s, cw, lo, hi, d, at, 2, 3 * q) for d in range(3)])
            for f in range(q):

                def beside(at, f=f):
                    if step == 0:
                        return layer_of(s, c0, lo, hi, f, at, 3, 0)
                    if at in places:
                        return ends1[f, places.index(at)]
                    return near[f, 0 if at < x // 2 else 1]

                base = None if step == 0 else ends0[f, j]
                states[step + 1][f, j] = turned(
                    base, section_weights[step], w, beside(at), beside(at - 1), beside(at + 1)
                )

    def rows_of(k, f, row):
        flat = states[k].reshape(q * 2 * EDGE * y, z)
        return flat[pl.ds(f * 2 * EDGE * y + row, 2 * EDGE, stride=y), :]

    def put(kind, at, rows):
        if kind == "z":
            slab[at : at + s.rows_z, :] = part[at : at + s.rows_z, :] + rows
        else:
            slab[at : at + EDGE, :] = rows[:EDGE]
            slab[at + s.ex - EDGE : at + s.ex, :] = rows[EDGE:]

    def layers_of(k):
        some = range(0 if k == 0 else 1, EDGE)
        return list(some) + [s.ex - 1 - a for a in some]

    def tile_of(k, f, a):
        return states[k][f, a if a < EDGE else a - s.ex + 2 * EDGE]

    slab_parts(s, rows_of, tile_of, layers_of, put)


WTOP, WPAD = 12, 40
BLOCK = slice(8, 32)


def assemble(s, c0, cw, lo, hi, below, above, pad, wind):
    q, x, y, z = s.q, s.x, s.y, s.z
    flat = pad.reshape(q * s.ep * WPAD, z)
    flat_wind = wind.reshape(3 * s.ex * 24, z)
    for f in range(q):
        for at in range(-3, x + 3):
            pad[f, at + 3, WTOP : WTOP + y, :] = layer_of(s, c0, lo, hi, f, at, 3, 0)
    for d in range(3):
        for at in range(-2, x + 2):
            wind[d, at + 2, 4 : 4 + y, :] = layer_of(s, cw, lo, hi, d, at, 2, 3 * q)
    for src, rows, start in zip((below, above), y_rows(s, q, 3), (WTOP - 3, WTOP + y)):
        for m, r, e, at in rows:
            count = x + 2 * e
            flat[pl.ds((m * s.ep + 3 - e) * WPAD + start + r, count, stride=WPAD), :] = src[at : at + count, :]
    for src, rows, start in zip((below, above), y_rows(s, 3, 2), (2, 4 + y)):
        for m, r, e, at in rows:
            count, at = x + 2 * e, at + s.rows_f
            flat_wind[pl.ds((m * s.ex + 2 - e) * 24 + start + r, count, stride=24), :] = src[at : at + count, :]


def edge_lanes(s, lane, width):
    return (lane < width) | (lane >= s.z - width)


def zpack_kernel(s, c0, cw, lo, hi, below, above, out, pad, wind):
    assemble(s, c0, cw, lo, hi, below, above, pad, wind)
    lane = lanes_of((24, s.z))
    keep = edge_lanes(s, lane, 3)
    for m in range(s.q + 3):
        total = None
        for a in range(s.ex):
            tile = pad[m, a + 1, BLOCK, :] if m < s.q else wind[m - s.q, a]
            part = pltpu.roll(jnp.where(keep, tile, 0.0), (6 * a + 3) % s.z, 1)
            total = part if total is None else total + part
        out[m] = total


def coarse_kernel(
    s, sides, c0, cw, lo, hi, below, above, zown, zin, out, pad0, pad1, pad2, wind, beyond, nearest
):
    q, x, y, z = s.q, s.x, s.y, s.z
    assemble(s, c0, cw, lo, hi, below, above, pad0, wind)
    pads = (pad0, pad1, pad2)
    lane = lanes_of((24, z))
    group = lane % 6
    from_low = group == 2
    from_high = group == 3
    exists = jnp.where(group < 3, sides[0, 0], sides[0, 1]).astype(F32)
    wind_z = scaled([zin[q + d] for d in range(3)])
    for f in range(q):
        beyond[0, f] = zin[f] * exists
        nearest[0, f] = zown[f]
    for step in range(3):
        src, fraction = pads[step], section_weights[step]
        flat = src.reshape(q * s.ep * WPAD, z)
        flat_wind = wind.reshape(3 * s.ex * 24, z)
        flat_beyond = beyond.reshape(3 * q * 24, z)
        skip, height = (0, 24) if step < 2 else (4, y)
        here = lanes_of((height, z))
        is_first, is_last = here == 0, here == z - 1

        def layer(a, packed, step=step, src=src, flat=flat, fraction=fraction, skip=skip, height=height):
            made = []
            if step < 2:
                w = scaled([wind[d, a] for d in range(3)])
            else:
                w = scaled([flat_wind[pl.ds((d * s.ex + a) * 24 + skip, height), :] for d in range(3)])
            for f in range(q):
                row = (f * s.ep + a + 1) * WPAD + 8 + skip

                def at_layer(of, layer, row, f=f):
                    return of[f, layer, BLOCK, :] if step < 2 else of.reshape(flat.shape)[pl.ds(row, height), :]

                center = at_layer(src, a + 1, row)
                ghost = pltpu.roll(flat_beyond[pl.ds((step * q + f) * 24 + skip, height), :], 2 * z - 6 * a - 3, 1)
                value = advanced(
                    None if step == 0 else at_layer(pad0, a + 1, row),
                    fraction,
                    w,
                    center,
                    at_layer(src, a, row - WPAD),
                    at_layer(src, a + 2, row + WPAD),
                    flat[pl.ds(row - 1, height), :],
                    flat[pl.ds(row + 1, height), :],
                    pltpu.roll(jnp.where(is_last, ghost, center), 1, 1),
                    pltpu.roll(jnp.where(is_first, ghost, center), z - 1, 1),
                )
                if step == 2:
                    out[f, a - 2] = value
                else:
                    pads[step + 1][f, a + 1, BLOCK, :] = value
                if step == 0:
                    made.append(packed[f] + pltpu.roll(jnp.where(is_first | is_last, value, 0.0), 6 * a + 3, 1))
            return tuple(made)

        begin, end = step, s.ex - step
        start = tuple(jnp.zeros((24, z), F32) for _ in range(q)) if step == 0 else ()
        packed = unrolled(begin, end, (end - begin) // 2, layer, start)
        if step == 2:
            break
        for f in range(q):
            if step == 0:
                nearest[1, f] = packed[f]
            ghost, near = beyond[step, f], nearest[step, f]
            value = advanced(
                None if step == 0 else beyond[0, f],
                fraction,
                wind_z,
                ghost,
                pltpu.roll(ghost, 6, 1),
                pltpu.roll(ghost, z - 6, 1),
                pltpu.roll(ghost, 1, 0),
                pltpu.roll(ghost, 23, 0),
                pltpu.roll(jnp.where(from_low, near, ghost), 1, 1),
                pltpu.roll(jnp.where(from_high, near, ghost), z - 1, 1),
            )
            beyond[step + 1, f] = value * exists


def fine_kernel(s, f0, fw, flo_there, fhi_there, slab, out, avg, *scratch):
    s1, s2, faces, ghost_rows, zface, flo, fhi, sems = scratch
    arrivals = [
        pltpu.make_async_copy(flo_there, flo, sems.at[4]),
        pltpu.make_async_copy(fhi_there, fhi, sems.at[5]),
    ]
    for move in arrivals:
        move.start()
    states = (None, s1, s2, s1)
    q, y, z, fx, fe = s.q, s.y, s.z, s.fx, s.fe
    layers = fx + 6
    rows = slice(TOP, TOP + y)
    r = lax.broadcasted_iota(jnp.int32, (z, 2 * z), 0)
    c = lax.broadcasted_iota(jnp.int32, (z, 2 * z), 1)
    near = c // 2
    far = near + 2 * (c % 2) - 1
    same = (far // s.sz == near // s.sz) & (far >= 0)
    to_fine = jnp.where(r == near, 0.75, jnp.where((r == far) & same, 0.25, 0.0)).astype(BF16)
    wide = times(slab[: s.rows_y, :], to_fine)
    ends = slab[s.rows_y : s.rows_y + s.ex, :]
    lane_x = lanes_of((s.ex, z))
    edge = (lane_x == 0) | (lane_x == z - 1)
    half = fe // 2
    for k in range(3):
        for f in range(q):
            for side in range(2):
                e = 4 * (q * k + f) + 2 * side + 1
                corner = jnp.where(edge, 0.25 * pltpu.roll(ends, z - e, 1), 0.0)
                first = (k * q + f) * s.ex
                here = faces.at[(k * q + f) * 2 + side]
                here[: s.ex, :] = wide[first : first + s.ex, side * z : side * z + z] + corner
                a = here[0:half, :]
                b = here[1 : half + 1, :]
                d = here[2 : half + 2, :]
                if k == 0:
                    flat, base, stride = ghost_rows, (2 * f + side) * fe, 1
                else:
                    flat, stride = states[k].reshape(q * layers * PAD, z), PAD
                    base = (f * layers + 1) * PAD + (TOP - 1 if side == 0 else TOP + y)
                flat[pl.ds(base, half, stride=2 * stride), :] = 0.25 * a + 0.75 * b
                flat[pl.ds(base + stride, half, stride=2 * stride), :] = 0.75 * b + 0.25 * d
    for f in range(q):
        at = s.rows_e + f * s.rows_z
        a = slab[at : at + s.sy, :]
        b = slab[at + 1 : at + 1 + s.sy, :]
        d = slab[at + 2 : at + 2 + s.sy, :]
        zface[pl.ds(f * y, s.sy, stride=2), :] = 0.25 * a + 0.75 * b
        zface[pl.ds(f * y + 1, s.sy, stride=2), :] = 0.75 * b + 0.25 * d
        a = zface[f * y : f * y + y, :]
        b = pltpu.roll(a, z - 2, 1)
        d = pltpu.roll(a, z - 4, 1)
        zface[f * y : f * y + y, :] = 0.25 * a + 0.75 * b
        zface[(q + f) * y : (q + f + 1) * y, :] = 0.75 * b + 0.25 * d
    lane = lanes_of((y, z))
    is_first, is_last = lane == 0, lane == z - 1
    row_in = lax.broadcasted_iota(jnp.int32, (y, z), 0)
    is_low, is_high = row_in == 0, row_in == y - 1
    flat_f0 = f0.reshape(q * fx * y, z)

    def pair_of_layers(k, t, inner):
        src = states[k]
        for odd in range(2):
            b = 2 * t + odd
            at = b - 2

            def field(f, at):
                return f0[f, at] if inner else layer_of(s, f0, flo, fhi, f, at, 3, 0)

            if inner:
                winds = [fw[d, at] for d in range(3)]
            else:
                winds = [layer_of(s, fw, flo, fhi, d, at, 2, 3 * q) for d in range(3)]
            w = scaled(winds)
            for f in range(q):
                if k == 0:
                    center, x_low, x_high = field(f, at), field(f, at - 1), field(f, at + 1)
                    if inner:
                        row = (f * fx + at) * y
                        y_low, y_high = flat_f0[pl.ds(row - 1, y), :], flat_f0[pl.ds(row + 1, y), :]
                    else:
                        y_low, y_high = pltpu.roll(center, 1, 0), pltpu.roll(center, y - 1, 0)
                    y_low = jnp.where(is_low, ghost_rows[pl.ds(2 * f * fe + b, 1), :], y_low)
                    y_high = jnp.where(is_high, ghost_rows[pl.ds((2 * f + 1) * fe + b, 1), :], y_high)
                    base = None
                else:
                    flat = src.reshape(q * layers * PAD, z)
                    row = (f * layers + b + 1) * PAD + TOP
                    center, x_low, x_high = src[f, b + 1, rows, :], src[f, b, rows, :], src[f, b + 2, rows, :]
                    y_low, y_high = flat[pl.ds(row - 1, y), :], flat[pl.ds(row + 1, y), :]
                    base = field(f, at)
                ghost = zface[(odd * q + f) * y : (odd * q + f + 1) * y, :]
                ghost = pltpu.roll(ghost, (2 * z - 2 * s.ex * k - 2 * t) if inner else -(2 * s.ex * k + 2 * t) % z, 1)
                value = advanced(
                    base,
                    section_weights[k],
                    w,
                    center,
                    x_low,
                    x_high,
                    y_low,
                    y_high,
                    pltpu.roll(jnp.where(is_last, ghost, center), 1, 1),
                    pltpu.roll(jnp.where(is_first, ghost, center), z - 1, 1),
                )
                states[k + 1][f, b + 1, rows, :] = value

    for move in arrivals:
        move.wait()
    moves = []
    for k in range(3):
        if k < 2:
            outer = 2 - k
            for t in list(range(outer)) + list(range(half - outer, half)):
                pair_of_layers(k, t, False)
            unrolled(outer, half - outer, 7 + k, lambda t, g, k=k: pair_of_layers(k, t, True))
            continue
        part = (half - 2) // 4
        for i in range(4):
            unrolled(1 + i * part, 1 + (i + 1) * part, 4, lambda t, g, k=k: pair_of_layers(k, t, True))
            begin, end = 2 * part * i, 2 * part * (i + 1)
            moves.append(pltpu.make_async_copy(s1.at[:, 3 + begin : 3 + end, rows], out.at[:, begin:end], sems.at[i]))
            moves[-1].start()
    rz = lax.broadcasted_iota(jnp.int32, (z, z), 0)
    cz = lax.broadcasted_iota(jnp.int32, (z, z), 1)
    flat = s1.reshape(q * layers * PAD, z)
    pairs_z = [jnp.where(cz == rz // 2 + odd * s.sz, 0.125, 0.0).astype(BF16) for odd in range(2)]
    for f in range(q):
        sums = []
        for odd in range(2):
            parts = []
            for p in range(s.x // 2):
                base = (f * layers + 3 + 4 * p + 2 * odd) * PAD + TOP
                part = None
                for more in (0, 1, PAD, PAD + 1):
                    piece = flat[pl.ds(base + more, y // 2, stride=2), :]
                    part = piece if part is None else part + piece
                parts.append(part)
            sums.append(times(jnp.concatenate(parts, axis=0), pairs_z[odd]))
        avg[f] = (sums[0] + sums[1]).reshape(s.x // 2, y // 2, z)
    for move in moves:
        move.wait()


def merge_kernel(s, c3, avg, out, made, sems):
    lane = lanes_of((s.sy, s.z))
    inside = (lane >= s.lz) & (lane < s.lz + s.sz)
    moves = []
    for f in range(s.q):
        for p in range(s.x // 2):
            both = avg[f, p]
            for odd in range(2):
                at = 2 * p + odd
                moved = pltpu.roll(both, s.lz if odd == 0 else s.z - s.lz, 1)
                made[f, at] = c3[f, at]
                made[f, at, s.ly : s.ly + s.sy, :] = jnp.where(inside, moved, c3[f, at, s.ly : s.ly + s.sy, :])
        moves.append(pltpu.make_async_copy(made.at[f], out.at[f], sems.at[f]))
        moves[-1].start()
    for move in moves:
        move.wait()


SHORT = pl.CostEstimate(flops=1, bytes_accessed=1, transcendentals=0)


def run(kernel, name, ins, outs, scratch, megabytes, spaces=None, cost=SHORT):
    spaces = spaces or [pltpu.VMEM] * len(ins)
    outs = [out if isinstance(out[0], tuple) else (out, pltpu.VMEM) for out in outs]
    ins = [i if space is pltpu.SMEM else pltpu.with_memory_space_constraint(i, space) for i, space in zip(ins, spaces)]
    return pl.pallas_call(
        kernel,
        out_shape=tuple(space(dims, F32) for dims, space in outs),
        in_specs=[pl.BlockSpec(memory_space=space) for space in spaces],
        out_specs=tuple(pl.BlockSpec(memory_space=space) for _, space in outs),
        scratch_shapes=scratch,
        compiler_params=pltpu.CompilerParams(vmem_limit_bytes=megabytes << 20),
        cost_estimate=cost,
        name=name,
    )(*ins)


def ring(array, axis, by):
    size = lax.axis_size(axis)
    return lax.ppermute(array, axis, [(i, (i + by) % size) for i in range(size)])


def move_by(array, amount, beside=None):
    size = lax.axis_size("gx")
    work, operands = beside or (lambda: (), ())
    if size <= 8:

        def branch(by, array, *operands):
            return array if by == 0 else ring(array, "gx", by), work(*operands)

        return lax.switch(amount, [functools.partial(branch, by) for by in range(size)], array, *operands)
    for bit in range((size - 1).bit_length()):
        array = jnp.where((amount >> bit) % 2 == 1, ring(array, "gx", 1 << bit), array)
    return array, work(*operands)


def z_columns(zown):
    size = lax.axis_size("gz")
    if size == 1:
        return zown
    if size == 2:
        return lax.ppermute(zown, "gz", [(0, 1), (1, 0)])
    below = lax.broadcasted_iota(jnp.int32, zown.shape, 2) % 6 < 3
    return jnp.where(below, ring(zown, "gz", 1), ring(zown, "gz", -1))


def pack(s, fields, wind, spare, name):
    return run(
        functools.partial(pack_kernel, s),
        name,
        [fields, wind],
        [(s.halo + spare, s.y, s.z)] * 2,
        [pltpu.SemaphoreType.DMA((4,))],
        1,
        [pltpu.HBM] * 2,
    )


def shards(coarse_fields, coarse_wind, fine_fields, fine_wind, fine_owner):
    s = Sizes(coarse_fields.shape, fine_fields.shape)
    q, x, y, z, fx = s.q, s.x, s.y, s.z, s.fx
    size = lax.axis_size("gx")
    offset = (fine_owner[0, 0, 0] - lax.axis_index("gx")) % size
    level = lax.axis_index("gz")
    neighbours = jnp.stack([level > 0, level < lax.axis_size("gz") - 1]).astype(jnp.int32).reshape(1, 2)
    cup, cdown = pack(s, coarse_fields, coarse_wind, 0, "pack_coarse")
    lo, hi = ring(cup, "gx", 1), ring(cdown, "gx", -1)
    part, near = run(
        functools.partial(inner_kernel, s),
        "inner",
        [coarse_fields, coarse_wind],
        [(s.slab, z), (q, 2, y, z)],
        [pltpu.VMEM((q, x, y, z), F32)] * 2,
        3,
    )
    fup, fdown = pack(s, fine_fields, fine_wind, 2, "pack_fine")
    fup, fdown, offset = lax.optimization_barrier((fup, fdown, offset))
    flo, fhi = ring(fup, "gx", 1), ring(fdown, "gx", -1)
    padded = [pltpu.VMEM((q, s.ep, WPAD, z), F32)]
    wind_rows = [pltpu.VMEM((3, s.ex, 24, z), F32)]

    coarse_fields, part, near = lax.optimization_barrier((coarse_fields, part, near))
    coarse_level = [coarse_fields, coarse_wind, lo, hi]
    yup, ydn = run(functools.partial(ypack_kernel, s), "ypack", coarse_level, [(s.rows_f + s.rows_w, z)] * 2, [], 1)
    yrows = [ring(yup, "gy", 1), ring(ydn, "gy", -1)]
    ends = [pltpu.VMEM((q, 2 * EDGE, y, z), F32)] * 3
    (slab,) = run(functools.partial(slab_kernel, s), "slab", coarse_level + [part, near], [(s.slab, z)], ends, 3)
    slab, _ = move_by(slab, (size - offset) % size)
    yrows, slab, flo, fhi = lax.optimization_barrier((yrows, slab, flo, fhi))
    kernel = functools.partial(zpack_kernel, s)
    (zown,) = run(kernel, "zpack", coarse_level + yrows, [(q + 3, 24, z)], padded + wind_rows, 4)
    zin = z_columns(zown)
    layers = fx + 6
    fine_next, averaged = run(
        functools.partial(fine_kernel, s),
        "fine",
        [fine_fields, fine_wind, flo, fhi, slab],
        [((q, fx, y, z), pltpu.HBM), (q, x // 2, y // 2, z)],
        [
            pltpu.VMEM((q, layers, PAD, z), F32),
            pltpu.VMEM((q, layers, PAD, z), F32),
            pltpu.VMEM((6 * q, s.ep, z), F32),
            pltpu.VMEM((2 * q * s.fe, z), F32),
            pltpu.VMEM((2 * q * y, z), F32),
            pltpu.VMEM(flo.shape, F32),
            pltpu.VMEM(fhi.shape, F32),
            pltpu.SemaphoreType.DMA((6,)),
        ],
        9,
        [pltpu.VMEM, pltpu.VMEM, pltpu.HBM, pltpu.HBM, pltpu.VMEM],
    )

    def coarse(*ins):
        cost = pl.CostEstimate(flops=40_000_000, bytes_accessed=4_000_000, transcendentals=0)
        columns = [pltpu.VMEM((3, q, 24, z), F32), pltpu.VMEM((2, q, 24, z), F32)]
        spaces = [pltpu.SMEM] + [pltpu.VMEM] * (len(ins) - 1)
        kernel = functools.partial(coarse_kernel, s)
        return run(kernel, "coarse", ins, [(q, x, y, z)], padded * 3 + wind_rows + columns, 9, spaces, cost)[0]

    averaged, state = move_by(averaged, offset, (coarse, (neighbours, *coarse_level, *yrows, zown, zin)))
    (coarse_next,) = run(
        functools.partial(merge_kernel, s),
        "merge",
        [state, averaged],
        [((q, x, y, z), pltpu.HBM)],
        [pltpu.VMEM((q, x, y, z), F32), pltpu.SemaphoreType.DMA((q,))],
        2,
    )
    return coarse_next, fine_next


def solution(mesh):
    spec = P(None, "gx", "gy", "gz")
    return jax.shard_map(
        shards,
        mesh=mesh,
        in_specs=(spec, spec, spec, spec, P("gx", "gy", "gz")),
        out_specs=(spec, spec),
        check_vma=False,
    )
```

profile of v0, /device:TPU:0, one launch (start us, length us, event | category | flops | bytes accessed | tf_op | source)
XLA Modules:
  0.0 63.3 jit_solution(5037725678134842765)
XLA Ops:
  0.6 1.0 %pack_coarse.1 = (f32[18,16,128]{2,1,0:T(8,128)S(1)}, f32[18,16,128]{2,1,0:T(8,128)S(1)}) custom-call(f32[4,16,16,128]{3,2,1,0:T(8,128)} %c0.4, f32[3,16,16,128]{3,2,1,0:T(8,128)} %cw.7), custom_call_target="tpu_custom_call" | custom-call | flops 1 | bytes 1 | tf_op jit(solution)/shard_map/pack_coarse/pallas_call | solution.py:555
  1.6 3.1 %collective-permute-start.6 = (f32[18,16,128]{2,1,0:T(8,128)S(1)}, f32[18,16,128]{2,1,0:T(8,128)S(1)}, u32[]{:S(2)}, u32[]{:S(2)}) collective-permute-start(f32[18,16,128]{2,1,0:T(8,128)S(1)} %get-tuple-element.160), channel_id=1, source_target_pairs={{0,8},{8,16},{16,24},{24,0},{1,9},{9,17},{17,25},{25,1},{2,10},{10... | collective-permute-start | bytes 442376 | tf_op jit(solution)/shard_map/ppermute | solution.py:569
  4.7 0.0 copy-start
  4.7 0.0 copy-start.1
  4.7 2.1 %collective-permute-start.7 = (f32[18,16,128]{2,1,0:T(8,128)S(1)}, f32[18,16,128]{2,1,0:T(8,128)S(1)}, u32[]{:S(2)}, u32[]{:S(2)}) collective-permute-start(f32[18,16,128]{2,1,0:T(8,128)S(1)} %get-tuple-element.161), channel_id=1, source_target_pairs={{0,24},{8,0},{16,8},{24,16},{1,25},{9,1},{17,9},{25,17},{2,26},{10... | collective-permute-start | bytes 442376 | tf_op jit(solution)/shard_map/ppermute | solution.py:569
  6.8 1.6 %pack_fine.1 = (f32[20,16,128]{2,1,0:T(8,128)}, f32[20,16,128]{2,1,0:T(8,128)S(1)}) custom-call(f32[4,32,16,128]{3,2,1,0:T(8,128)} %f0.1, f32[3,32,16,128]{3,2,1,0:T(8,128)} %fw.1), custom_call_target="tpu_custom_call" | custom-call | flops 1 | bytes 1 | tf_op jit(solution)/shard_map/pack_fine/pallas_call | solution.py:555
  9.1 0.1 collective-permute-start.10
  9.2 3.8 %collective-permute-start.11 = (f32[20,16,128]{2,1,0:T(8,128)S(1)}, f32[20,16,128]{2,1,0:T(8,128)}, u32[]{:S(2)}, u32[]{:S(2)}) collective-permute-start(f32[20,16,128]{2,1,0:T(8,128)S(1)} %get-tuple-element.167), channel_id=1, source_target_pairs={{0,24},{8,0},{16,8},{24,16},{1,25},{9,1},{17,9},{25,17},{2,26},{10... | collective-permute-start | bytes 491528 | tf_op jit(solution)/shard_map/ppermute | solution.py:569
  13.0 0.0 copy-done
  13.0 0.0 copy-done.1
  13.0 2.5 %inner.1 = (f32[304,128]{1,0:T(8,128)S(1)}, f32[4,2,16,128]{3,2,1,0:T(8,128)S(1)}) custom-call(f32[4,16,16,128]{3,2,1,0:T(8,128)S(1)} %copy-done, f32[3,16,16,128]{3,2,1,0:T(8,128)S(1)} %copy-done.1), custom_call_target="tpu_custom_call" | custom-call | flops 1 | bytes 1 | tf_op jit(solution)/shard_map/inner/pallas_call | solution.py:555
  15.5 0.0 collective-permute-done.6.lo
  15.6 0.0 collective-permute-done.7.hi
  15.6 0.8 %ypack.1 = (f32[318,128]{1,0:T(8,128)}, f32[318,128]{1,0:T(8,128)}) custom-call(f32[4,16,16,128]{3,2,1,0:T(8,128)S(1)} %copy-done, f32[3,16,16,128]{3,2,1,0:T(8,128)S(1)} %copy-done.1, f32[18,16,128]{2,1,0:T(8,128)S(1)} %collective-permute-done.6.lo, f32[18,16,128]{2,1,0:T(8,128)S(1)} %collective-permute-done.7.hi), custom_call_target="tpu_custom_call" | custom-call | flops 1 | bytes 1 | tf_op jit(solution)/shard_map/ypack/pallas_call | solution.py:555
  16.4 0.0 collective-permute-start.8
  16.4 1.7 %collective-permute-start.9 = (f32[318,128]{1,0:T(8,128)}, f32[318,128]{1,0:T(8,128)S(1)}, u32[]{:S(2)}, u32[]{:S(2)}) collective-permute-start(f32[318,128]{1,0:T(8,128)} %get-tuple-element.163), channel_id=1, source_target_pairs={{0,6},{2,0},{4,2},{6,4},{1,7},{3,1},{5,3},{7,5},{8,14},{10,8},{12,... | collective-permute-start | bytes 488456 | tf_op jit(solution)/shard_map/ppermute | solution.py:569
  18.1 1.8 %slab.1 = f32[304,128]{1,0:T(8,128)S(1)} custom-call(f32[4,16,16,128]{3,2,1,0:T(8,128)S(1)} %copy-done, f32[3,16,16,128]{3,2,1,0:T(8,128)S(1)} %copy-done.1, f32[18,16,128]{2,1,0:T(8,128)S(1)} %collective-permute-done.6.lo, f32[18,16,128]{2,1,0:T(8,128)S(1)} %collective-permute-done.7.hi, f32[304,128]{1,0:T(8,128)S(1)} %get-tuple-element.164.part, ...), custom_call_target="tpu_custom_call" | custom-call | flops 1 | bytes 1 | tf_op jit(solution)/shard_map/slab/pallas_call | solution.py:555
  19.9 0.0 copy-start.3
  19.9 8.7 %conditional.2 = (f32[304,128]{1,0:T(8,128)S(1)}) conditional(s32[]{:T(128)} %clamp.7, f32[304,128]{1,0:T(8,128)S(1)} %slab.1, f32[304,128]{1,0:T(8,128)S(1)} %slab.1, f32[304,128]{1,0:T(8,128)S(1)} %slab.1, f32[304,128]{1,0:T(8,128)S(1)} %slab.1), branch_computations={%region_0.1_spmd, %region_1.2_spmd, %region_2.3_spmd, %region_3.4_... | conditional | bytes 933936 | solution.py:580
  20.0 0.1 collective-permute-start.1
  20.0 8.6 %collective-permute-done.1 = f32[304,128]{1,0:T(8,128)S(1)} collective-permute-done((f32[304,128]{1,0:T(8,128)S(1)}, f32[304,128]{1,0:T(8,128)S(1)}, u32[]{:S(2)}, u32[]{:S(2)}) %collective-permute-start.1) | collective-permute-done | bytes 155680 | tf_op jit(solution)/shard_map/cond/branch_2_fun/ppermute | solution.py:569
  28.7 0.0 copy-start.4
  28.7 0.7 %copy-done.4 = f32[304,128]{1,0:T(8,128)} copy-done((f32[304,128]{1,0:T(8,128)}, f32[304,128]{1,0:T(8,128)S(1)}, u32[]{:S(2)}) %copy-start.4) | copy-done | bytes 155672
  29.4 0.0 copy-start.2
  29.4 0.0 copy-start.5
  29.4 0.0 collective-permute-done.10.flo_there
  29.4 0.0 collective-permute-done.11.fhi_there
  29.4 0.0 collective-permute-done.8.below
  29.4 0.0 collective-permute-done.9.above
  29.4 0.5 zpack.1
  29.9 0.7 %collective-permute-start.12 = (f32[7,24,128]{2,1,0:T(8,128)S(1)}, f32[7,24,128]{2,1,0:T(8,128)S(1)}, u32[]{:S(2)}, u32[]{:S(2)}) collective-permute-start(f32[7,24,128]{2,1,0:T(8,128)S(1)} %zpack.1), channel_id=1, source_target_pairs={{0,1},{1,0},{2,3},{3,2},{4,5},{5,4},{6,7},{7,6},{8,9},{9,8},{10,11... | collective-permute-start | bytes 258056 | tf_op jit(solution)/shard_map/ppermute | solution.py:591
  30.6 0.1 add_convert_fusion
  30.7 0.0 copy-done.3
  30.7 0.0 copy-done.2
  30.7 0.0 copy-done.5
  30.7 17.2 %fine.1 = (f32[4,32,16,128]{3,2,1,0:T(8,128)}, f32[4,8,8,128]{3,2,1,0:T(8,128)S(1)}) custom-call(f32[4,32,16,128]{3,2,1,0:T(8,128)S(1)} %copy-done.2, f32[3,32,16,128]{3,2,1,0:T(8,128)S(1)} %copy-done.3, f32[20,16,128]{2,1,0:T(8,128)} %collective-permute-done.10.flo_there, f32[20,16,128]{2,1,0:T(8,128)} %collective-permute-done.11.fhi_there, ...), custom_call_target="tpu_custom_call" | custom-call | flops 1 | bytes 1 | tf_op jit(solution)/shard_map/fine/pallas_call | solution.py:555
  47.9 0.0 collective-permute-done.12
  47.9 14.4 %conditional.3 = (f32[4,8,8,128]{3,2,1,0:T(8,128)S(1)}, f32[4,16,16,128]{3,2,1,0:T(8,128)S(1)}) conditional(s32[]{:T(128)} %clamp.6, (s32[1,2]{1,0:T(1,128)S(1)}, f32[4,16,16,128]{3,2,1,0:T(8,128)S(1)}, f32[3,16,16,128]{3,2,1,0:T(8,128)S(1)}, f32[18,16,128]{2,1,0:T(8,128)S(1)}, f32[18,16,128]{2,1,0:T(8,128)S(1)}, ...), branch_computations={%region_4.5_spmd, %region_5.6_spmd, %region_6.7_spmd, %region_7.8_... | conditional | flops 40000000 | bytes 4786488 | solution.py:580
  48.1 0.1 collective-permute-start.4
  48.2 13.8 %coarse.6 = f32[4,16,16,128]{3,2,1,0:T(8,128)S(1)} custom-call(s32[1,2]{1,0:T(1,128)S(1)} %get-tuple-element.110.sides, f32[4,16,16,128]{3,2,1,0:T(8,128)S(1)} %get-tuple-element.111.c0, f32[3,16,16,128]{3,2,1,0:T(8,128)S(1)} %get-tuple-element.112.cw, f32[18,16,128]{2,1,0:T(8,128)S(1)} %get-tuple-element.113.lo, f32[18,16,128]{2,1,0:T(8,128)S(1)} %get-tuple-element.114.hi, ...), custom_call_target="tpu_custom_call" | custom-call | flops 40000000 | bytes 4000000 | tf_op jit(solution)/shard_map/cond/branch_2_fun/coarse/pallas_call | solution.py:555
  62.0 0.0 collective-permute-done.4
  62.3 0.9 %merge.1 = f32[4,16,16,128]{3,2,1,0:T(8,128)} custom-call(f32[4,16,16,128]{3,2,1,0:T(8,128)S(1)} %get-tuple-element.174.c3, f32[4,8,8,128]{3,2,1,0:T(8,128)S(1)} %get-tuple-element.175.avg), custom_call_target="tpu_custom_call" | custom-call | flops 1 | bytes 1 | tf_op jit(solution)/shard_map/merge/pallas_call | solution.py:555
  (2 shorter events, 0.0 us)
Async XLA Ops:
  1.6 13.9 %collective-permute-start.6 = (f32[18,16,128]{2,1,0:T(8,128)S(1)}, f32[18,16,128]{2,1,0:T(8,128)S(1)}, u32[]{:S(2)}, u32[]{:S(2)}) collective-permute-start(f32[18,16,128]{2,1,0:T(8,128)S(1)} %get-tuple-element.160), channel_id=1, source_target_pairs={{0,8},{8,16},{16,24},{24,0},{1,9},{9,17},{17,25},{25,1},{2,10},{10... | collective-permute-start | bytes 442376 | tf_op jit(solution)/shard_map/ppermute | solution.py:569
  4.7 8.3 %copy-start = (f32[4,16,16,128]{3,2,1,0:T(8,128)S(1)}, f32[4,16,16,128]{3,2,1,0:T(8,128)}, u32[]{:S(2)}) copy-start(f32[4,16,16,128]{3,2,1,0:T(8,128)} %c0.4) | copy-start | bytes 1572868
  4.7 8.3 %copy-start.1 = (f32[3,16,16,128]{3,2,1,0:T(8,128)S(1)}, f32[3,16,16,128]{3,2,1,0:T(8,128)}, u32[]{:S(2)}) copy-start(f32[3,16,16,128]{3,2,1,0:T(8,128)} %cw.7) | copy-start | bytes 1179652
  4.7 10.9 %collective-permute-start.7 = (f32[18,16,128]{2,1,0:T(8,128)S(1)}, f32[18,16,128]{2,1,0:T(8,128)S(1)}, u32[]{:S(2)}, u32[]{:S(2)}) collective-permute-start(f32[18,16,128]{2,1,0:T(8,128)S(1)} %get-tuple-element.161), channel_id=1, source_target_pairs={{0,24},{8,0},{16,8},{24,16},{1,25},{9,1},{17,9},{25,17},{2,26},{10... | collective-permute-start | bytes 442376 | tf_op jit(solution)/shard_map/ppermute | solution.py:569
  9.1 20.2 %collective-permute-start.10 = (f32[20,16,128]{2,1,0:T(8,128)}, f32[20,16,128]{2,1,0:T(8,128)}, u32[]{:S(2)}, u32[]{:S(2)}) collective-permute-start(f32[20,16,128]{2,1,0:T(8,128)} %get-tuple-element.166), channel_id=1, source_target_pairs={{0,8},{8,16},{16,24},{24,0},{1,9},{9,17},{17,25},{25,1},{2,10},{10... | collective-permute-start | bytes 491528 | tf_op jit(solution)/shard_map/ppermute | solution.py:569
  9.2 20.2 %collective-permute-start.11 = (f32[20,16,128]{2,1,0:T(8,128)S(1)}, f32[20,16,128]{2,1,0:T(8,128)}, u32[]{:S(2)}, u32[]{:S(2)}) collective-permute-start(f32[20,16,128]{2,1,0:T(8,128)S(1)} %get-tuple-element.167), channel_id=1, source_target_pairs={{0,24},{8,0},{16,8},{24,16},{1,25},{9,1},{17,9},{25,17},{2,26},{10... | collective-permute-start | bytes 491528 | tf_op jit(solution)/shard_map/ppermute | solution.py:569
  16.4 13.0 %collective-permute-start.8 = (f32[318,128]{1,0:T(8,128)}, f32[318,128]{1,0:T(8,128)S(1)}, u32[]{:S(2)}, u32[]{:S(2)}) collective-permute-start(f32[318,128]{1,0:T(8,128)} %get-tuple-element.162), channel_id=1, source_target_pairs={{0,2},{2,4},{4,6},{6,0},{1,3},{3,5},{5,7},{7,1},{8,10},{10,12},{12... | collective-permute-start | bytes 488456 | tf_op jit(solution)/shard_map/ppermute | solution.py:569
  16.4 13.0 %collective-permute-start.9 = (f32[318,128]{1,0:T(8,128)}, f32[318,128]{1,0:T(8,128)S(1)}, u32[]{:S(2)}, u32[]{:S(2)}) collective-permute-start(f32[318,128]{1,0:T(8,128)} %get-tuple-element.163), channel_id=1, source_target_pairs={{0,6},{2,0},{4,2},{6,4},{1,7},{3,1},{5,3},{7,5},{8,14},{10,8},{12,... | collective-permute-start | bytes 488456 | tf_op jit(solution)/shard_map/ppermute | solution.py:569
  19.9 10.7 %copy-start.3 = (f32[3,32,16,128]{3,2,1,0:T(8,128)S(1)}, f32[3,32,16,128]{3,2,1,0:T(8,128)}, u32[]{:S(2)}) copy-start(f32[3,32,16,128]{3,2,1,0:T(8,128)} %fw.1) | copy-start | bytes 2359300
  20.0 8.7 %collective-permute-start.1 = (f32[304,128]{1,0:T(8,128)S(1)}, f32[304,128]{1,0:T(8,128)S(1)}, u32[]{:S(2)}, u32[]{:S(2)}) collective-permute-start(f32[304,128]{1,0:T(8,128)S(1)} %param.2), channel_id=1, source_target_pairs={{0,16},{8,24},{16,0},{24,8},{1,17},{9,25},{17,1},{25,9},{2,18},{10... | collective-permute-start | bytes 466952 | tf_op jit(solution)/shard_map/cond/branch_2_fun/ppermute | solution.py:569
  28.7 0.7 %copy-start.4 = (f32[304,128]{1,0:T(8,128)}, f32[304,128]{1,0:T(8,128)S(1)}, u32[]{:S(2)}) copy-start(f32[304,128]{1,0:T(8,128)S(1)} %get-tuple-element.185.slab) | copy-start | bytes 466948
  29.4 1.3 %copy-start.2 = (f32[4,32,16,128]{3,2,1,0:T(8,128)S(1)}, f32[4,32,16,128]{3,2,1,0:T(8,128)}, u32[]{:S(2)}) copy-start(f32[4,32,16,128]{3,2,1,0:T(8,128)} %f0.1) | copy-start | bytes 3145732
  29.4 1.3 %copy-start.5 = (f32[304,128]{1,0:T(8,128)S(1)}, f32[304,128]{1,0:T(8,128)}, u32[]{:S(2)}) copy-start(f32[304,128]{1,0:T(8,128)} %copy-done.4) | copy-start | bytes 466948
  29.9 18.0 %collective-permute-start.12 = (f32[7,24,128]{2,1,0:T(8,128)S(1)}, f32[7,24,128]{2,1,0:T(8,128)S(1)}, u32[]{:S(2)}, u32[]{:S(2)}) collective-permute-start(f32[7,24,128]{2,1,0:T(8,128)S(1)} %zpack.1), channel_id=1, source_target_pairs={{0,1},{1,0},{2,3},{3,2},{4,5},{5,4},{6,7},{7,6},{8,9},{9,8},{10,11... | collective-permute-start | bytes 258056 | tf_op jit(solution)/shard_map/ppermute | solution.py:591
  48.1 13.9 %collective-permute-start.4 = (f32[4,8,8,128]{3,2,1,0:T(8,128)S(1)}, f32[4,8,8,128]{3,2,1,0:T(8,128)S(1)}, u32[]{:S(2)}, u32[]{:S(2)}) collective-permute-start(f32[4,8,8,128]{3,2,1,0:T(8,128)S(1)} %get-tuple-element.109), channel_id=1, source_target_pairs={{0,16},{8,24},{16,0},{24,8},{1,17},{9,25},{17,1},{25,9},{2,18},{10... | collective-permute-start | bytes 393224 | tf_op jit(solution)/shard_map/cond/branch_2_fun/ppermute | solution.py:569
where the time goes:
time: 63.2 us; the launch traced here: 63.3 us
  Pallas kernels  40.2 us (64%)
  starting transfers between devices  11.6 us (18%)
  waiting for transfers between devices  8.64 us (14%)
  between operations  1.61 us (3%)
  local copies, waits for them, and re-layouts  0.71 us (1%)
    pallas_call x9, Pallas kernels, run(): pl.pallas_call(kernel, out_shape=tuple((space(dims, F32) for dims, space...  40.2 us
    ppermute x8, starting transfers between devices, ring(): lax.ppermute(array, axis, [(i, (i + by) % size) for i in range(size)])  10.9 us
    ppermute x8, waiting for transfers between devices, ring(): lax.ppermute(array, axis, [(i, (i + by) % size) for i in range(size)])  8.64 us
  transfers between devices with their start and end apart: 9, of which 1 were waited for; matrix products, arithmetic and copies ran while one was open for 0% of the time, Pallas kernels for 60%

commit v1 on v0

--- a/solution.py
+++ b/solution.py
@@ -51,10 +51,12 @@
     return [w * (-0.5 / diffusion) for w in wind]
 
 
-def advanced(base, fraction, wind, center, x_low, x_high, y_low, y_high, z_low, z_high):
-    total = (x_high + x_low) + wind[0] * (x_high - x_low)
-    total = total + ((y_high + y_low) + wind[1] * (y_high - y_low))
-    total = total + ((z_high + z_low) + wind[2] * (z_high - z_low))
+def along(wind, low, high):
+    return (high + low) + wind * (high - low)
+
+
+def advanced(base, fraction, wind, center, x_low, x_high, y_low, y_high, vertical):
+    total = (vertical + along(wind[0], x_low, x_high)) + along(wind[1], y_low, y_high)
     if base is None:
         return center * (1.0 - 6.0 * diffusion * fraction) + total * (diffusion * fraction)
     return (base - center * (6.0 * diffusion * fraction)) + total * (diffusion * fraction)
@@ -135,8 +137,7 @@
         x_high,
         pltpu.roll(center, 1, 0),
         pltpu.roll(center, y - 1, 0),
-        pltpu.roll(center, 1, 1),
-        pltpu.roll(center, z - 1, 1),
+        along(wind[2], pltpu.roll(center, 1, 1), pltpu.roll(center, z - 1, 1)),
     )
 
 
@@ -303,7 +304,7 @@
 
 
 def coarse_kernel(
-    s, sides, c0, cw, lo, hi, below, above, zown, zin, out, pad0, pad1, pad2, wind, beyond, nearest
+    s, sides, c0, cw, lo, hi, below, above, zown, zin, out, pad0, pad1, pad2, wind, beyond, nearest, vertical
 ):
     q, x, y, z = s.q, s.x, s.y, s.z
     assemble(s, c0, cw, lo, hi, below, above, pad0, wind)
@@ -326,47 +327,60 @@
         here = lanes_of((height, z))
         is_first, is_last = here == 0, here == z - 1
 
-        def layer(a, packed, step=step, src=src, flat=flat, fraction=fraction, skip=skip, height=height):
+        def at_layer(of, f, layer, by, step=step, skip=skip, height=height):
+            if step < 2 and not by:
+                return of[f, layer, BLOCK, :]
+            row = (f * s.ep + layer) * WPAD + 8 + skip + by
+            return of.reshape(q * s.ep * WPAD, z)[pl.ds(row, height), :]
+
+        def wind_at(d, a, step=step, skip=skip, height=height):
+            if step < 2:
+                return wind[d, a]
+            return flat_wind[pl.ds((d * s.ex + a) * 24 + skip, height), :]
+
+        def vertical_of(a, packed, step=step, src=src, skip=skip, height=height):
+            (w,) = scaled([wind_at(2, a)])
             made = []
-            if step < 2:
-                w = scaled([wind[d, a] for d in range(3)])
-            else:
-                w = scaled([flat_wind[pl.ds((d * s.ex + a) * 24 + skip, height), :] for d in range(3)])
             for f in range(q):
-                row = (f * s.ep + a + 1) * WPAD + 8 + skip
-
-                def at_layer(of, layer, row, f=f):
-                    return of[f, layer, BLOCK, :] if step < 2 else of.reshape(flat.shape)[pl.ds(row, height), :]
-
-                center = at_layer(src, a + 1, row)
+                center = at_layer(src, f, a + 1, 0)
                 ghost = pltpu.roll(flat_beyond[pl.ds((step * q + f) * 24 + skip, height), :], 2 * z - 6 * a - 3, 1)
+                vertical[f, a, :height, :] = along(
+                    w,
+                    pltpu.roll(jnp.where(is_last, ghost, center), 1, 1),
+                    pltpu.roll(jnp.where(is_first, ghost, center), z - 1, 1),
+                )
+                if step == 1:
+                    made.append(packed[f] + pltpu.roll(jnp.where(is_first | is_last, center, 0.0), 6 * a + 3, 1))
+            return tuple(made)
+
+        def layer(a, carry, step=step, src=src, fraction=fraction, height=height):
+            w = scaled([wind_at(d, a) for d in range(2)])
+            for f in range(q):
                 value = advanced(
-                    None if step == 0 else at_layer(pad0, a + 1, row),
+                    None if step == 0 else at_layer(pad0, f, a + 1, 0),
                     fraction,
                     w,
-                    center,
-                    at_layer(src, a, row - WPAD),
-                    at_layer(src, a + 2, row + WPAD),
-                    flat[pl.ds(row - 1, height), :],
-                    flat[pl.ds(row + 1, height), :],
-                    pltpu.roll(jnp.where(is_last, ghost, center), 1, 1),
-                    pltpu.roll(jnp.where(is_first, ghost, center), z - 1, 1),
+                    at_layer(src, f, a + 1, 0),
+                    at_layer(src, f, a, 0),
+                    at_layer(src, f, a + 2, 0),
+                    at_layer(src, f, a + 1, -1),
+                    at_layer(src, f, a + 1, 1),
+                    vertical[f, a, :height, :],
                 )
                 if step == 2:
                     out[f, a - 2] = value
                 else:
                     pads[step + 1][f, a + 1, BLOCK, :] = value
-                if step == 0:
-                    made.append(packed[f] + pltpu.roll(jnp.where(is_first | is_last, value, 0.0), 6 * a + 3, 1))
-            return tuple(made)
+            return carry
 
         begin, end = step, s.ex - step
-        start = tuple(jnp.zeros((24, z), F32) for _ in range(q)) if step == 0 else ()
-        packed = unrolled(begin, end, (end - begin) // 2, layer, start)
+        start = tuple(jnp.zeros((24, z), F32) for _ in range(q)) if step == 1 else ()
+        packed = unrolled(begin, end, 4, vertical_of, start)
+        unrolled(begin, end, 4, layer)
         if step == 2:
             break
         for f in range(q):
-            if step == 0:
+            if step == 1:
                 nearest[1, f] = packed[f]
             ghost, near = beyond[step, f], nearest[step, f]
             value = advanced(
@@ -378,14 +392,17 @@
                 pltpu.roll(ghost, z - 6, 1),
                 pltpu.roll(ghost, 1, 0),
                 pltpu.roll(ghost, 23, 0),
-                pltpu.roll(jnp.where(from_low, near, ghost), 1, 1),
-                pltpu.roll(jnp.where(from_high, near, ghost), z - 1, 1),
+                along(
+                    wind_z[2],
+                    pltpu.roll(jnp.where(from_low, near, ghost), 1, 1),
+                    pltpu.roll(jnp.where(from_high, near, ghost), z - 1, 1),
+                ),
             )
             beyond[step + 1, f] = value * exists
 
 
 def fine_kernel(s, f0, fw, flo_there, fhi_there, slab, out, avg, *scratch):
-    s1, s2, faces, ghost_rows, zface, flo, fhi, sems = scratch
+    s1, s2, faces, ghost_rows, zface, flo, fhi, vertical, sems = scratch
     arrivals = [
         pltpu.make_async_copy(flo_there, flo, sems.at[4]),
         pltpu.make_async_copy(fhi_there, fhi, sems.at[5]),
@@ -443,23 +460,35 @@
     is_low, is_high = row_in == 0, row_in == y - 1
     flat_f0 = f0.reshape(q * fx * y, z)
 
+    def field(f, at, inner):
+        return f0[f, at] if inner else layer_of(s, f0, flo, fhi, f, at, 3, 0)
+
+    def wind_of(d, at, inner):
+        return fw[d, at] if inner else layer_of(s, fw, flo, fhi, d, at, 2, 3 * q)
+
+    def vertical_of(k, t, inner):
+        for odd in range(2):
+            b = 2 * t + odd
+            (w,) = scaled([wind_of(2, b - 2, inner)])
+            for f in range(q):
+                center = field(f, b - 2, inner) if k == 0 else states[k][f, b + 1, rows, :]
+                ghost = zface[(odd * q + f) * y : (odd * q + f + 1) * y, :]
+                ghost = pltpu.roll(ghost, (2 * z - 2 * s.ex * k - 2 * t) if inner else -(2 * s.ex * k + 2 * t) % z, 1)
+                vertical[f, b] = along(
+                    w,
+                    pltpu.roll(jnp.where(is_last, ghost, center), 1, 1),
+                    pltpu.roll(jnp.where(is_first, ghost, center), z - 1, 1),
+                )
+
     def pair_of_layers(k, t, inner):
         src = states[k]
         for odd in range(2):
             b = 2 * t + odd
             at = b - 2
-
-            def field(f, at):
-                return f0[f, at] if inner else layer_of(s, f0, flo, fhi, f, at, 3, 0)
-
-            if inner:
-                winds = [fw[d, at] for d in range(3)]
-            else:
-                winds = [layer_of(s, fw, flo, fhi, d, at, 2, 3 * q) for d in range(3)]
-            w = scaled(winds)
+            w = scaled([wind_of(d, at, inner) for d in range(2)])
             for f in range(q):
                 if k == 0:
-                    center, x_low, x_high = field(f, at), field(f, at - 1), field(f, at + 1)
+                    center, x_low, x_high = field(f, at, inner), field(f, at - 1, inner), field(f, at + 1, inner)
                     if inner:
                         row = (f * fx + at) * y
                         y_low, y_high = flat_f0[pl.ds(row - 1, y), :], flat_f0[pl.ds(row + 1, y), :]
@@ -473,20 +502,9 @@
                     row = (f * layers + b + 1) * PAD + TOP
                     center, x_low, x_high = src[f, b + 1, rows, :], src[f, b, rows, :], src[f, b + 2, rows, :]
                     y_low, y_high = flat[pl.ds(row - 1, y), :], flat[pl.ds(row + 1, y), :]
-                    base = field(f, at)
-                ghost = zface[(odd * q + f) * y : (odd * q + f + 1) * y, :]
-                ghost = pltpu.roll(ghost, (2 * z - 2 * s.ex * k - 2 * t) if inner else -(2 * s.ex * k + 2 * t) % z, 1)
+                    base = field(f, at, inner)
                 value = advanced(
-                    base,
-                    section_weights[k],
-                    w,
-                    center,
-                    x_low,
-                    x_high,
-                    y_low,
-                    y_high,
-                    pltpu.roll(jnp.where(is_last, ghost, center), 1, 1),
-                    pltpu.roll(jnp.where(is_first, ghost, center), z - 1, 1),
+                    base, section_weights[k], w, center, x_low, x_high, y_low, y_high, vertical[f, b]
                 )
                 states[k + 1][f, b + 1, rows, :] = value
 
@@ -494,18 +512,20 @@
         move.wait()
     moves = []
     for k in range(3):
-        if k < 2:
-            outer = 2 - k
-            for t in list(range(outer)) + list(range(half - outer, half)):
-                pair_of_layers(k, t, False)
-            unrolled(outer, half - outer, 7 + k, lambda t, g, k=k: pair_of_layers(k, t, True))
-            continue
-        part = (half - 2) // 4
-        for i in range(4):
-            unrolled(1 + i * part, 1 + (i + 1) * part, 4, lambda t, g, k=k: pair_of_layers(k, t, True))
-            begin, end = 2 * part * i, 2 * part * (i + 1)
-            moves.append(pltpu.make_async_copy(s1.at[:, 3 + begin : 3 + end, rows], out.at[:, begin:end], sems.at[i]))
-            moves[-1].start()
+        outer = (2, 1, 1)[k]
+        for part in (vertical_of, pair_of_layers):
+            if k < 2:
+                for t in list(range(outer)) + list(range(half - outer, half)):
+                    part(k, t, False)
+            if k == 2 and part is pair_of_layers:
+                break
+            unrolled(outer, half - outer, 2, lambda t, g, k=k, part=part: part(k, t, True))
+    quarter = (half - 2) // 4
+    for i in range(4):
+        unrolled(1 + i * quarter, 1 + (i + 1) * quarter, 2, lambda t, g: pair_of_layers(2, t, True))
+        begin, end = 2 * quarter * i, 2 * quarter * (i + 1)
+        moves.append(pltpu.make_async_copy(s1.at[:, 3 + begin : 3 + end, rows], out.at[:, begin:end], sems.at[i]))
+        moves[-1].start()
     rz = lax.broadcasted_iota(jnp.int32, (z, z), 0)
     cz = lax.broadcasted_iota(jnp.int32, (z, z), 1)
     flat = s1.reshape(q * layers * PAD, z)
@@ -653,18 +673,19 @@
             pltpu.VMEM((2 * q * y, z), F32),
             pltpu.VMEM(flo.shape, F32),
             pltpu.VMEM(fhi.shape, F32),
+            pltpu.VMEM((q, s.fe, y, z), F32),
             pltpu.SemaphoreType.DMA((6,)),
         ],
-        9,
+        10,
         [pltpu.VMEM, pltpu.VMEM, pltpu.HBM, pltpu.HBM, pltpu.VMEM],
     )
 
     def coarse(*ins):
         cost = pl.CostEstimate(flops=40_000_000, bytes_accessed=4_000_000, transcendentals=0)
-        columns = [pltpu.VMEM((3, q, 24, z), F32), pltpu.VMEM((2, q, 24, z), F32)]
+        columns = [pltpu.VMEM((3, q, 24, z), F32), pltpu.VMEM((2, q, 24, z), F32), pltpu.VMEM((q, s.ex, 24, z), F32)]
         spaces = [pltpu.SMEM] + [pltpu.VMEM] * (len(ins) - 1)
         kernel = functools.partial(coarse_kernel, s)
-        return run(kernel, "coarse", ins, [(q, x, y, z)], padded * 3 + wind_rows + columns, 9, spaces, cost)[0]
+        return run(kernel, "coarse", ins, [(q, x, y, z)], padded * 3 + wind_rows + columns, 11, spaces, cost)[0]
 
     averaged, state = move_by(averaged, offset, (coarse, (neighbours, *coarse_level, *yrows, zown, zin)))
     (coarse_next,) = run(

time: 63.2 us -> 49.1 us (0.78)
  Pallas kernels: 40.2 us -> 25.7 us
  waiting for transfers between devices: 8.64 us -> 9.48 us
    pallas_call x9, Pallas kernels: 40.2 us -> 25.7 us  [run(): pl.pallas_call(kernel, out_shape=tuple((space(dims, F32) for dims, space...]
    ppermute x8, waiting for transfers between devices: 8.64 us -> 9.48 us  [ring(): lax.ppermute(array, axis, [(i, (i + by) % size) for i in range(size)])]
  transfers between devices with their start and end apart: 9 -> 9, of which waited for: 1 -> 2; matrix products, arithmetic and copies ran while one was open for 0% -> 0% of each run, Pallas kernels for 60% -> 47%
where the time goes in v1:
time: 49.1 us; the launch traced here: 49 us
  Pallas kernels  25.7 us (52%)
  starting transfers between devices  11.6 us (24%)
  waiting for transfers between devices  9.48 us (19%)
  between operations  1.43 us (3%)
  local copies, waits for them, and re-layouts  0.71 us (1%)
    pallas_call x9, Pallas kernels, run(): pl.pallas_call(kernel, out_shape=tuple((space(dims, F32) for dims, space...  25.7 us
    ppermute x8, starting transfers between devices, ring(): lax.ppermute(array, axis, [(i, (i + by) % size) for i in range(size)])  10.9 us
    ppermute x8, waiting for transfers between devices, ring(): lax.ppermute(array, axis, [(i, (i + by) % size) for i in range(size)])  9.48 us
  transfers between devices with their start and end apart: 9, of which 2 were waited for; matrix products, arithmetic and copies ran while one was open for 0% of the time, Pallas kernels for 47%

profile of v1, /device:TPU:0, one launch (start us, length us, event | category | flops | bytes accessed | tf_op | source)
XLA Modules:
  0.0 49.0 jit_solution(2187644027520886576)
XLA Ops:
  0.6 1.0 %pack_coarse.1 = (f32[18,16,128]{2,1,0:T(8,128)S(1)}, f32[18,16,128]{2,1,0:T(8,128)S(1)}) custom-call(f32[4,16,16,128]{3,2,1,0:T(8,128)} %c0.4, f32[3,16,16,128]{3,2,1,0:T(8,128)} %cw.7), custom_call_target="tpu_custom_call" | custom-call | flops 1 | bytes 1 | tf_op jit(solution)/shard_map/pack_coarse/pallas_call | solution.py:575
  1.6 3.1 %collective-permute-start.6 = (f32[18,16,128]{2,1,0:T(8,128)S(1)}, f32[18,16,128]{2,1,0:T(8,128)S(1)}, u32[]{:S(2)}, u32[]{:S(2)}) collective-permute-start(f32[18,16,128]{2,1,0:T(8,128)S(1)} %get-tuple-element.160), channel_id=1, source_target_pairs={{0,8},{8,16},{16,24},{24,0},{1,9},{9,17},{17,25},{25,1},{2,10},{10... | collective-permute-start | bytes 442376 | tf_op jit(solution)/shard_map/ppermute | solution.py:589
  4.7 0.0 copy-start
  4.7 0.0 copy-start.1
  4.7 2.1 %collective-permute-start.7 = (f32[18,16,128]{2,1,0:T(8,128)S(1)}, f32[18,16,128]{2,1,0:T(8,128)S(1)}, u32[]{:S(2)}, u32[]{:S(2)}) collective-permute-start(f32[18,16,128]{2,1,0:T(8,128)S(1)} %get-tuple-element.161), channel_id=1, source_target_pairs={{0,24},{8,0},{16,8},{24,16},{1,25},{9,1},{17,9},{25,17},{2,26},{10... | collective-permute-start | bytes 442376 | tf_op jit(solution)/shard_map/ppermute | solution.py:589
  6.8 1.6 %pack_fine.1 = (f32[20,16,128]{2,1,0:T(8,128)}, f32[20,16,128]{2,1,0:T(8,128)S(1)}) custom-call(f32[4,32,16,128]{3,2,1,0:T(8,128)} %f0.1, f32[3,32,16,128]{3,2,1,0:T(8,128)} %fw.1), custom_call_target="tpu_custom_call" | custom-call | flops 1 | bytes 1 | tf_op jit(solution)/shard_map/pack_fine/pallas_call | solution.py:575
  9.1 0.1 collective-permute-start.10
  9.2 3.8 %collective-permute-start.11 = (f32[20,16,128]{2,1,0:T(8,128)S(1)}, f32[20,16,128]{2,1,0:T(8,128)}, u32[]{:S(2)}, u32[]{:S(2)}) collective-permute-start(f32[20,16,128]{2,1,0:T(8,128)S(1)} %get-tuple-element.167), channel_id=1, source_target_pairs={{0,24},{8,0},{16,8},{24,16},{1,25},{9,1},{17,9},{25,17},{2,26},{10... | collective-permute-start | bytes 491528 | tf_op jit(solution)/shard_map/ppermute | solution.py:589
  13.0 0.0 copy-done
  13.0 0.0 copy-done.1
  13.0 2.5 %inner.1 = (f32[304,128]{1,0:T(8,128)S(1)}, f32[4,2,16,128]{3,2,1,0:T(8,128)S(1)}) custom-call(f32[4,16,16,128]{3,2,1,0:T(8,128)S(1)} %copy-done, f32[3,16,16,128]{3,2,1,0:T(8,128)S(1)} %copy-done.1), custom_call_target="tpu_custom_call" | custom-call | flops 1 | bytes 1 | tf_op jit(solution)/shard_map/inner/pallas_call | solution.py:575
  15.6 0.0 collective-permute-done.6.lo
  15.6 0.0 collective-permute-done.7.hi
  15.6 0.8 %ypack.1 = (f32[318,128]{1,0:T(8,128)}, f32[318,128]{1,0:T(8,128)}) custom-call(f32[4,16,16,128]{3,2,1,0:T(8,128)S(1)} %copy-done, f32[3,16,16,128]{3,2,1,0:T(8,128)S(1)} %copy-done.1, f32[18,16,128]{2,1,0:T(8,128)S(1)} %collective-permute-done.6.lo, f32[18,16,128]{2,1,0:T(8,128)S(1)} %collective-permute-done.7.hi), custom_call_target="tpu_custom_call" | custom-call | flops 1 | bytes 1 | tf_op jit(solution)/shard_map/ypack/pallas_call | solution.py:575
  16.4 0.0 collective-permute-start.8
  16.4 1.7 %collective-permute-start.9 = (f32[318,128]{1,0:T(8,128)}, f32[318,128]{1,0:T(8,128)S(1)}, u32[]{:S(2)}, u32[]{:S(2)}) collective-permute-start(f32[318,128]{1,0:T(8,128)} %get-tuple-element.163), channel_id=1, source_target_pairs={{0,6},{2,0},{4,2},{6,4},{1,7},{3,1},{5,3},{7,5},{8,14},{10,8},{12,... | collective-permute-start | bytes 488456 | tf_op jit(solution)/shard_map/ppermute | solution.py:589
  18.2 1.8 %slab.1 = f32[304,128]{1,0:T(8,128)S(1)} custom-call(f32[4,16,16,128]{3,2,1,0:T(8,128)S(1)} %copy-done, f32[3,16,16,128]{3,2,1,0:T(8,128)S(1)} %copy-done.1, f32[18,16,128]{2,1,0:T(8,128)S(1)} %collective-permute-done.6.lo, f32[18,16,128]{2,1,0:T(8,128)S(1)} %collective-permute-done.7.hi, f32[304,128]{1,0:T(8,128)S(1)} %get-tuple-element.164.part, ...), custom_call_target="tpu_custom_call" | custom-call | flops 1 | bytes 1 | tf_op jit(solution)/shard_map/slab/pallas_call | solution.py:575
  19.9 0.0 copy-start.3
  20.0 8.7 %conditional.2 = (f32[304,128]{1,0:T(8,128)S(1)}) conditional(s32[]{:T(128)} %clamp.7, f32[304,128]{1,0:T(8,128)S(1)} %slab.1, f32[304,128]{1,0:T(8,128)S(1)} %slab.1, f32[304,128]{1,0:T(8,128)S(1)} %slab.1, f32[304,128]{1,0:T(8,128)S(1)} %slab.1), branch_computations={%region_0.1_spmd, %region_1.2_spmd, %region_2.3_spmd, %region_3.4_... | conditional | bytes 933936 | solution.py:600
  20.0 0.1 collective-permute-start.1
  20.1 8.6 %collective-permute-done.1 = f32[304,128]{1,0:T(8,128)S(1)} collective-permute-done((f32[304,128]{1,0:T(8,128)S(1)}, f32[304,128]{1,0:T(8,128)S(1)}, u32[]{:S(2)}, u32[]{:S(2)}) %collective-permute-start.1) | collective-permute-done | bytes 155680 | tf_op jit(solution)/shard_map/cond/branch_2_fun/ppermute | solution.py:589
  28.7 0.0 copy-start.4
  28.7 0.7 %copy-done.4 = f32[304,128]{1,0:T(8,128)} copy-done((f32[304,128]{1,0:T(8,128)}, f32[304,128]{1,0:T(8,128)S(1)}, u32[]{:S(2)}) %copy-start.4) | copy-done | bytes 155672
  29.4 0.0 copy-start.2
  29.4 0.0 copy-start.5
  29.4 0.0 collective-permute-done.10.flo_there
  29.4 0.0 collective-permute-done.11.fhi_there
  29.4 0.0 collective-permute-done.8.below
  29.4 0.0 collective-permute-done.9.above
  29.4 0.5 %zpack.1 = f32[7,24,128]{2,1,0:T(8,128)S(1)} custom-call(f32[4,16,16,128]{3,2,1,0:T(8,128)S(1)} %copy-done, f32[3,16,16,128]{3,2,1,0:T(8,128)S(1)} %copy-done.1, f32[18,16,128]{2,1,0:T(8,128)S(1)} %collective-permute-done.6.lo, f32[18,16,128]{2,1,0:T(8,128)S(1)} %collective-permute-done.7.hi, f32[318,128]{1,0:T(8,128)S(1)} %collective-permute-done.8.below, ...), custom_call_target="tpu_custom_call" | custom-call | flops 1 | bytes 1 | tf_op jit(solution)/shard_map/zpack/pallas_call | solution.py:575
  29.9 0.7 %collective-permute-start.12 = (f32[7,24,128]{2,1,0:T(8,128)S(1)}, f32[7,24,128]{2,1,0:T(8,128)S(1)}, u32[]{:S(2)}, u32[]{:S(2)}) collective-permute-start(f32[7,24,128]{2,1,0:T(8,128)S(1)} %zpack.1), channel_id=1, source_target_pairs={{0,1},{1,0},{2,3},{3,2},{4,5},{5,4},{6,7},{7,6},{8,9},{9,8},{10,11... | collective-permute-start | bytes 258056 | tf_op jit(solution)/shard_map/ppermute | solution.py:611
  30.6 0.1 add_convert_fusion
  30.7 0.0 copy-done.3
  30.7 0.0 copy-done.2
  30.7 0.0 copy-done.5
  30.7 9.4 %fine.1 = (f32[4,32,16,128]{3,2,1,0:T(8,128)}, f32[4,8,8,128]{3,2,1,0:T(8,128)S(1)}) custom-call(f32[4,32,16,128]{3,2,1,0:T(8,128)S(1)} %copy-done.2, f32[3,32,16,128]{3,2,1,0:T(8,128)S(1)} %copy-done.3, f32[20,16,128]{2,1,0:T(8,128)} %collective-permute-done.10.flo_there, f32[20,16,128]{2,1,0:T(8,128)} %collective-permute-done.11.fhi_there, ...), custom_call_target="tpu_custom_call" | custom-call | flops 1 | bytes 1 | tf_op jit(solution)/shard_map/fine/pallas_call | solution.py:575
  40.1 0.0 collective-permute-done.12
  40.1 8.0 %conditional.3 = (f32[4,8,8,128]{3,2,1,0:T(8,128)S(1)}, f32[4,16,16,128]{3,2,1,0:T(8,128)S(1)}) conditional(s32[]{:T(128)} %clamp.6, (s32[1,2]{1,0:T(1,128)S(1)}, f32[4,16,16,128]{3,2,1,0:T(8,128)S(1)}, f32[3,16,16,128]{3,2,1,0:T(8,128)S(1)}, f32[18,16,128]{2,1,0:T(8,128)S(1)}, f32[18,16,128]{2,1,0:T(8,128)S(1)}, ...), branch_computations={%region_4.5_spmd, %region_5.6_spmd, %region_6.7_spmd, %region_7.8_... | conditional | flops 40000000 | bytes 4786488 | solution.py:600
  40.1 0.1 collective-permute-start.4
  40.2 7.0 %coarse.6 = f32[4,16,16,128]{3,2,1,0:T(8,128)S(1)} custom-call(s32[1,2]{1,0:T(1,128)S(1)} %get-tuple-element.110.sides, f32[4,16,16,128]{3,2,1,0:T(8,128)S(1)} %get-tuple-element.111.c0, f32[3,16,16,128]{3,2,1,0:T(8,128)S(1)} %get-tuple-element.112.cw, f32[18,16,128]{2,1,0:T(8,128)S(1)} %get-tuple-element.113.lo, f32[18,16,128]{2,1,0:T(8,128)S(1)} %get-tuple-element.114.hi, ...), custom_call_target="tpu_custom_call" | custom-call | flops 40000000 | bytes 4000000 | tf_op jit(solution)/shard_map/cond/branch_2_fun/coarse/pallas_call | solution.py:575
  47.3 0.9 %collective-permute-done.4 = f32[4,8,8,128]{3,2,1,0:T(8,128)S(1)} collective-permute-done((f32[4,8,8,128]{3,2,1,0:T(8,128)S(1)}, f32[4,8,8,128]{3,2,1,0:T(8,128)S(1)}, u32[]{:S(2)}, u32[]{:S(2)}) %collective-permute-start.4) | collective-permute-done | bytes 131104 | tf_op jit(solution)/shard_map/cond/branch_2_fun/ppermute | solution.py:589
  48.1 0.9 %merge.1 = f32[4,16,16,128]{3,2,1,0:T(8,128)} custom-call(f32[4,16,16,128]{3,2,1,0:T(8,128)S(1)} %get-tuple-element.174.c3, f32[4,8,8,128]{3,2,1,0:T(8,128)S(1)} %get-tuple-element.175.avg), custom_call_target="tpu_custom_call" | custom-call | flops 1 | bytes 1 | tf_op jit(solution)/shard_map/merge/pallas_call | solution.py:575
  (2 shorter events, 0.0 us)
Async XLA Ops:
  1.6 13.9 %collective-permute-start.6 = (f32[18,16,128]{2,1,0:T(8,128)S(1)}, f32[18,16,128]{2,1,0:T(8,128)S(1)}, u32[]{:S(2)}, u32[]{:S(2)}) collective-permute-start(f32[18,16,128]{2,1,0:T(8,128)S(1)} %get-tuple-element.160), channel_id=1, source_target_pairs={{0,8},{8,16},{16,24},{24,0},{1,9},{9,17},{17,25},{25,1},{2,10},{10... | collective-permute-start | bytes 442376 | tf_op jit(solution)/shard_map/ppermute | solution.py:589
  4.7 8.3 %copy-start = (f32[4,16,16,128]{3,2,1,0:T(8,128)S(1)}, f32[4,16,16,128]{3,2,1,0:T(8,128)}, u32[]{:S(2)}) copy-start(f32[4,16,16,128]{3,2,1,0:T(8,128)} %c0.4) | copy-start | bytes 1572868
  4.7 8.3 %copy-start.1 = (f32[3,16,16,128]{3,2,1,0:T(8,128)S(1)}, f32[3,16,16,128]{3,2,1,0:T(8,128)}, u32[]{:S(2)}) copy-start(f32[3,16,16,128]{3,2,1,0:T(8,128)} %cw.7) | copy-start | bytes 1179652
  4.7 10.9 %collective-permute-start.7 = (f32[18,16,128]{2,1,0:T(8,128)S(1)}, f32[18,16,128]{2,1,0:T(8,128)S(1)}, u32[]{:S(2)}, u32[]{:S(2)}) collective-permute-start(f32[18,16,128]{2,1,0:T(8,128)S(1)} %get-tuple-element.161), channel_id=1, source_target_pairs={{0,24},{8,0},{16,8},{24,16},{1,25},{9,1},{17,9},{25,17},{2,26},{10... | collective-permute-start | bytes 442376 | tf_op jit(solution)/shard_map/ppermute | solution.py:589
  9.1 20.2 %collective-permute-start.10 = (f32[20,16,128]{2,1,0:T(8,128)}, f32[20,16,128]{2,1,0:T(8,128)}, u32[]{:S(2)}, u32[]{:S(2)}) collective-permute-start(f32[20,16,128]{2,1,0:T(8,128)} %get-tuple-element.166), channel_id=1, source_target_pairs={{0,8},{8,16},{16,24},{24,0},{1,9},{9,17},{17,25},{25,1},{2,10},{10... | collective-permute-start | bytes 491528 | tf_op jit(solution)/shard_map/ppermute | solution.py:589
  9.2 20.2 %collective-permute-start.11 = (f32[20,16,128]{2,1,0:T(8,128)S(1)}, f32[20,16,128]{2,1,0:T(8,128)}, u32[]{:S(2)}, u32[]{:S(2)}) collective-permute-start(f32[20,16,128]{2,1,0:T(8,128)S(1)} %get-tuple-element.167), channel_id=1, source_target_pairs={{0,24},{8,0},{16,8},{24,16},{1,25},{9,1},{17,9},{25,17},{2,26},{10... | collective-permute-start | bytes 491528 | tf_op jit(solution)/shard_map/ppermute | solution.py:589
  16.4 13.0 %collective-permute-start.8 = (f32[318,128]{1,0:T(8,128)}, f32[318,128]{1,0:T(8,128)S(1)}, u32[]{:S(2)}, u32[]{:S(2)}) collective-permute-start(f32[318,128]{1,0:T(8,128)} %get-tuple-element.162), channel_id=1, source_target_pairs={{0,2},{2,4},{4,6},{6,0},{1,3},{3,5},{5,7},{7,1},{8,10},{10,12},{12... | collective-permute-start | bytes 488456 | tf_op jit(solution)/shard_map/ppermute | solution.py:589
  16.4 13.0 %collective-permute-start.9 = (f32[318,128]{1,0:T(8,128)}, f32[318,128]{1,0:T(8,128)S(1)}, u32[]{:S(2)}, u32[]{:S(2)}) collective-permute-start(f32[318,128]{1,0:T(8,128)} %get-tuple-element.163), channel_id=1, source_target_pairs={{0,6},{2,0},{4,2},{6,4},{1,7},{3,1},{5,3},{7,5},{8,14},{10,8},{12,... | collective-permute-start | bytes 488456 | tf_op jit(solution)/shard_map/ppermute | solution.py:589
  19.9 10.7 %copy-start.3 = (f32[3,32,16,128]{3,2,1,0:T(8,128)S(1)}, f32[3,32,16,128]{3,2,1,0:T(8,128)}, u32[]{:S(2)}) copy-start(f32[3,32,16,128]{3,2,1,0:T(8,128)} %fw.1) | copy-start | bytes 2359300
  20.0 8.7 %collective-permute-start.1 = (f32[304,128]{1,0:T(8,128)S(1)}, f32[304,128]{1,0:T(8,128)S(1)}, u32[]{:S(2)}, u32[]{:S(2)}) collective-permute-start(f32[304,128]{1,0:T(8,128)S(1)} %param.2), channel_id=1, source_target_pairs={{0,16},{8,24},{16,0},{24,8},{1,17},{9,25},{17,1},{25,9},{2,18},{10... | collective-permute-start | bytes 466952 | tf_op jit(solution)/shard_map/cond/branch_2_fun/ppermute | solution.py:589
  28.7 0.7 %copy-start.4 = (f32[304,128]{1,0:T(8,128)}, f32[304,128]{1,0:T(8,128)S(1)}, u32[]{:S(2)}) copy-start(f32[304,128]{1,0:T(8,128)S(1)} %get-tuple-element.185.slab) | copy-start | bytes 466948
  29.4 1.3 %copy-start.2 = (f32[4,32,16,128]{3,2,1,0:T(8,128)S(1)}, f32[4,32,16,128]{3,2,1,0:T(8,128)}, u32[]{:S(2)}) copy-start(f32[4,32,16,128]{3,2,1,0:T(8,128)} %f0.1) | copy-start | bytes 3145732
  29.4 1.3 %copy-start.5 = (f32[304,128]{1,0:T(8,128)S(1)}, f32[304,128]{1,0:T(8,128)}, u32[]{:S(2)}) copy-start(f32[304,128]{1,0:T(8,128)} %copy-done.4) | copy-start | bytes 466948
  29.9 10.2 %collective-permute-start.12 = (f32[7,24,128]{2,1,0:T(8,128)S(1)}, f32[7,24,128]{2,1,0:T(8,128)S(1)}, u32[]{:S(2)}, u32[]{:S(2)}) collective-permute-start(f32[7,24,128]{2,1,0:T(8,128)S(1)} %zpack.1), channel_id=1, source_target_pairs={{0,1},{1,0},{2,3},{3,2},{4,5},{5,4},{6,7},{7,6},{8,9},{9,8},{10,11... | collective-permute-start | bytes 258056 | tf_op jit(solution)/shard_map/ppermute | solution.py:611
  40.1 8.0 %collective-permute-start.4 = (f32[4,8,8,128]{3,2,1,0:T(8,128)S(1)}, f32[4,8,8,128]{3,2,1,0:T(8,128)S(1)}, u32[]{:S(2)}, u32[]{:S(2)}) collective-permute-start(f32[4,8,8,128]{3,2,1,0:T(8,128)S(1)} %get-tuple-element.109), channel_id=1, source_target_pairs={{0,16},{8,24},{16,0},{24,8},{1,17},{9,25},{17,1},{25,9},{2,18},{10... | collective-permute-start | bytes 393224 | tf_op jit(solution)/shard_map/cond/branch_2_fun/ppermute | solution.py:589

commit v2 on v0

--- a/solution.py
+++ b/solution.py
@@ -47,17 +47,19 @@
     return jnp.dot(high, matrix, preferred_element_type=F32) + jnp.dot(low, matrix, preferred_element_type=F32)
 
 
-def scaled(wind):
-    return [w * (-0.5 / diffusion) for w in wind]
-
-
-def advanced(base, fraction, wind, center, x_low, x_high, y_low, y_high, z_low, z_high):
-    total = (x_high + x_low) + wind[0] * (x_high - x_low)
-    total = total + ((y_high + y_low) + wind[1] * (y_high - y_low))
-    total = total + ((z_high + z_low) + wind[2] * (z_high - z_low))
+def coefficients(fraction, wind):
+    out = []
+    for w in wind:
+        turned_by = w * (-0.5 * fraction)
+        out += [diffusion * fraction + turned_by, diffusion * fraction - turned_by]
+    return out
+
+
+def advanced(base, fraction, co, center, x_low, x_high, y_low, y_high, z_low, z_high):
+    along = (co[0] * x_high + co[1] * x_low) + (co[2] * y_high + co[3] * y_low) + (co[4] * z_high + co[5] * z_low)
     if base is None:
-        return center * (1.0 - 6.0 * diffusion * fraction) + total * (diffusion * fraction)
-    return (base - center * (6.0 * diffusion * fraction)) + total * (diffusion * fraction)
+        return center * (1.0 - 6.0 * diffusion * fraction) + along
+    return (base - center * (6.0 * diffusion * fraction)) + along
 
 
 def layer_of(s, own, low, high, member, at, width, first):
@@ -185,13 +187,13 @@
         src, dst = states[step], states[step + 1]
 
         def layer(j, carry, step=step, src=src, dst=dst):
-            w = scaled([cw[d, j] for d in range(3)])
+            w = coefficients(section_weights[step], [cw[d, j] for d in range(3)])
             for f in range(q):
                 base = None if step == 0 else c0[f, j]
                 dst[f, j] = turned(base, section_weights[step], w, src[f, j], src[f, j - 1], src[f, j + 1])
             return carry
 
-        unrolled(step + 1, x - 1 - step, 7 if step == 0 else 6, layer)
+        unrolled(step + 1, x - 1 - step, 2, layer)
     for f in range(q):
         near[f, 0] = state1[f, EDGE - 2]
         near[f, 1] = state1[f, x + 1 - EDGE]
@@ -225,7 +227,7 @@
                 for f in range(q):
                     ends2[f, j] = jnp.zeros((y, z), F32)
                 continue
-            w = scaled([layer_of(s, cw, lo, hi, d, at, 2, 3 * q) for d in range(3)])
+            w = coefficients(section_weights[step], [layer_of(s, cw, lo, hi, d, at, 2, 3 * q) for d in range(3)])
             for f in range(q):
 
                 def beside(at, f=f):
@@ -313,7 +315,7 @@
     from_low = group == 2
     from_high = group == 3
     exists = jnp.where(group < 3, sides[0, 0], sides[0, 1]).astype(F32)
-    wind_z = scaled([zin[q + d] for d in range(3)])
+    wind_z = [zin[q + d] for d in range(3)]
     for f in range(q):
         beyond[0, f] = zin[f] * exists
         nearest[0, f] = zown[f]
@@ -326,43 +328,53 @@
         here = lanes_of((height, z))
         is_first, is_last = here == 0, here == z - 1
 
-        def layer(a, packed, step=step, src=src, flat=flat, fraction=fraction, skip=skip, height=height):
-            made = []
-            if step < 2:
-                w = scaled([wind[d, a] for d in range(3)])
-            else:
-                w = scaled([flat_wind[pl.ds((d * s.ex + a) * 24 + skip, height), :] for d in range(3)])
+        def two_layers(t, packed, step=step, src=src, flat=flat, fraction=fraction, skip=skip, height=height):
+            first = step + 2 * t
+            packed = list(packed)
+            co = []
+            for a in (first, first + 1):
+                if step < 2:
+                    winds = [wind[d, a] for d in range(3)]
+                else:
+                    winds = [flat_wind[pl.ds((d * s.ex + a) * 24 + skip, height), :] for d in range(3)]
+                co.append(coefficients(fraction, winds))
             for f in range(q):
-                row = (f * s.ep + a + 1) * WPAD + 8 + skip
-
-                def at_layer(of, layer, row, f=f):
-                    return of[f, layer, BLOCK, :] if step < 2 else of.reshape(flat.shape)[pl.ds(row, height), :]
-
-                center = at_layer(src, a + 1, row)
-                ghost = pltpu.roll(flat_beyond[pl.ds((step * q + f) * 24 + skip, height), :], 2 * z - 6 * a - 3, 1)
-                value = advanced(
-                    None if step == 0 else at_layer(pad0, a + 1, row),
-                    fraction,
-                    w,
-                    center,
-                    at_layer(src, a, row - WPAD),
-                    at_layer(src, a + 2, row + WPAD),
-                    flat[pl.ds(row - 1, height), :],
-                    flat[pl.ds(row + 1, height), :],
-                    pltpu.roll(jnp.where(is_last, ghost, center), 1, 1),
-                    pltpu.roll(jnp.where(is_first, ghost, center), z - 1, 1),
-                )
-                if step == 2:
-                    out[f, a - 2] = value
-                else:
-                    pads[step + 1][f, a + 1, BLOCK, :] = value
-                if step == 0:
-                    made.append(packed[f] + pltpu.roll(jnp.where(is_first | is_last, value, 0.0), 6 * a + 3, 1))
-            return tuple(made)
-
-        begin, end = step, s.ex - step
+
+                def at_layer(of, layer, by=0, f=f):
+                    if step < 2 and not by:
+                        return of[f, layer, BLOCK, :]
+                    row = (f * s.ep + layer) * WPAD + 8 + skip + by
+                    return of.reshape(flat.shape)[pl.ds(row, height), :]
+
+                beside = flat_beyond[pl.ds((step * q + f) * 24 + skip, height), :]
+                row_of = [at_layer(src, first + i) for i in range(4)]
+                for i in range(2):
+                    a = first + i
+                    center = row_of[i + 1]
+                    ghost = pltpu.roll(beside, 2 * z - 6 * a - 3, 1)
+                    value = advanced(
+                        None if step == 0 else at_layer(pad0, a + 1),
+                        fraction,
+                        co[i],
+                        center,
+                        row_of[i],
+                        row_of[i + 2],
+                        at_layer(src, a + 1, -1),
+                        at_layer(src, a + 1, 1),
+                        pltpu.roll(jnp.where(is_last, ghost, center), 1, 1),
+                        pltpu.roll(jnp.where(is_first, ghost, center), z - 1, 1),
+                    )
+                    if step == 2:
+                        out[f, a - 2] = value
+                    else:
+                        pads[step + 1][f, a + 1, BLOCK, :] = value
+                    if step == 0:
+                        ends = jnp.where(is_first | is_last, value, 0.0)
+                        packed[f] = packed[f] + pltpu.roll(ends, 6 * a + 3, 1)
+            return tuple(packed)
+
         start = tuple(jnp.zeros((24, z), F32) for _ in range(q)) if step == 0 else ()
-        packed = unrolled(begin, end, (end - begin) // 2, layer, start)
+        packed = unrolled(0, s.ex // 2 - step, 2 + (step == 1), two_layers, start)
         if step == 2:
             break
         for f in range(q):
@@ -372,7 +384,7 @@
             value = advanced(
                 None if step == 0 else beyond[0, f],
                 fraction,
-                wind_z,
+                coefficients(fraction, wind_z),
                 ghost,
                 pltpu.roll(ghost, 6, 1),
                 pltpu.roll(ghost, z - 6, 1),
@@ -444,51 +456,52 @@
     flat_f0 = f0.reshape(q * fx * y, z)
 
     def pair_of_layers(k, t, inner):
-        src = states[k]
-        for odd in range(2):
-            b = 2 * t + odd
-            at = b - 2
-
-            def field(f, at):
-                return f0[f, at] if inner else layer_of(s, f0, flo, fhi, f, at, 3, 0)
-
+        src, fraction = states[k], section_weights[k]
+
+        def field(f, at):
+            return f0[f, at] if inner else layer_of(s, f0, flo, fhi, f, at, 3, 0)
+
+        co = []
+        for at in (2 * t - 2, 2 * t - 1):
             if inner:
                 winds = [fw[d, at] for d in range(3)]
             else:
                 winds = [layer_of(s, fw, flo, fhi, d, at, 2, 3 * q) for d in range(3)]
-            w = scaled(winds)
-            for f in range(q):
+            co.append(coefficients(fraction, winds))
+        for f in range(q):
+            if k == 0:
+                row_of = [field(f, 2 * t - 3 + i) for i in range(4)]
+            else:
+                row_of = [src[f, 2 * t + i, rows, :] for i in range(4)]
+            for odd in range(2):
+                b = 2 * t + odd
+                center = row_of[odd + 1]
                 if k == 0:
-                    center, x_low, x_high = field(f, at), field(f, at - 1), field(f, at + 1)
                     if inner:
-                        row = (f * fx + at) * y
+                        row = (f * fx + b - 2) * y
                         y_low, y_high = flat_f0[pl.ds(row - 1, y), :], flat_f0[pl.ds(row + 1, y), :]
                     else:
                         y_low, y_high = pltpu.roll(center, 1, 0), pltpu.roll(center, y - 1, 0)
                     y_low = jnp.where(is_low, ghost_rows[pl.ds(2 * f * fe + b, 1), :], y_low)
                     y_high = jnp.where(is_high, ghost_rows[pl.ds((2 * f + 1) * fe + b, 1), :], y_high)
-                    base = None
                 else:
                     flat = src.reshape(q * layers * PAD, z)
                     row = (f * layers + b + 1) * PAD + TOP
-                    center, x_low, x_high = src[f, b + 1, rows, :], src[f, b, rows, :], src[f, b + 2, rows, :]
                     y_low, y_high = flat[pl.ds(row - 1, y), :], flat[pl.ds(row + 1, y), :]
-                    base = field(f, at)
                 ghost = zface[(odd * q + f) * y : (odd * q + f + 1) * y, :]
                 ghost = pltpu.roll(ghost, (2 * z - 2 * s.ex * k - 2 * t) if inner else -(2 * s.ex * k + 2 * t) % z, 1)
-                value = advanced(
-                    base,
-                    section_weights[k],
-                    w,
+                states[k + 1][f, b + 1, rows, :] = advanced(
+                    None if k == 0 else field(f, b - 2),
+                    fraction,
+                    co[odd],
                     center,
-                    x_low,
-                    x_high,
+                    row_of[odd],
+                    row_of[odd + 2],
                     y_low,
                     y_high,
                     pltpu.roll(jnp.where(is_last, ghost, center), 1, 1),
                     pltpu.roll(jnp.where(is_first, ghost, center), z - 1, 1),
                 )
-                states[k + 1][f, b + 1, rows, :] = value
 
     for move in arrivals:
         move.wait()
@@ -498,11 +511,11 @@
             outer = 2 - k
             for t in list(range(outer)) + list(range(half - outer, half)):
                 pair_of_layers(k, t, False)
-            unrolled(outer, half - outer, 7 + k, lambda t, g, k=k: pair_of_layers(k, t, True))
+            unrolled(outer, half - outer, 2, lambda t, g, k=k: pair_of_layers(k, t, True))
             continue
         part = (half - 2) // 4
         for i in range(4):
-            unrolled(1 + i * part, 1 + (i + 1) * part, 4, lambda t, g, k=k: pair_of_layers(k, t, True))
+            unrolled(1 + i * part, 1 + (i + 1) * part, 2, lambda t, g, k=k: pair_of_layers(k, t, True))
             begin, end = 2 * part * i, 2 * part * (i + 1)
             moves.append(pltpu.make_async_copy(s1.at[:, 3 + begin : 3 + end, rows], out.at[:, begin:end], sems.at[i]))
             moves[-1].start()

time: 63.2 us -> 47.1 us (0.75)
  Pallas kernels: 40.2 us -> 24.2 us
  starting transfers between devices: 11.6 us -> 12.8 us
  waiting for transfers between devices: 8.64 us -> 7.73 us
    pallas_call x9, Pallas kernels: 40.2 us -> 24.2 us  [run(): pl.pallas_call(kernel, out_shape=tuple((space(dims, F32) for dims, space...]
    ppermute x8, starting transfers between devices: 10.9 us -> 11.9 us  [ring(): lax.ppermute(array, axis, [(i, (i + by) % size) for i in range(size)])]
    ppermute x8, waiting for transfers between devices: 8.64 us -> 7.73 us  [ring(): lax.ppermute(array, axis, [(i, (i + by) % size) for i in range(size)])]
  transfers between devices with their start and end apart: 9 -> 9, of which waited for: 1 -> 1; matrix products, arithmetic and copies ran while one was open for 0% -> 0% of each run, Pallas kernels for 60% -> 46%
where the time goes in v2:
time: 47.1 us; the launch traced here: 47 us
  Pallas kernels  24.2 us (51%)
  starting transfers between devices  12.8 us (27%)
  waiting for transfers between devices  7.73 us (16%)
  between operations  1.43 us (3%)
  local copies, waits for them, and re-layouts  0.71 us (2%)
    pallas_call x9, Pallas kernels, run(): pl.pallas_call(kernel, out_shape=tuple((space(dims, F32) for dims, space...  24.2 us
    ppermute x8, starting transfers between devices, ring(): lax.ppermute(array, axis, [(i, (i + by) % size) for i in range(size)])  11.9 us
    ppermute x8, waiting for transfers between devices, ring(): lax.ppermute(array, axis, [(i, (i + by) % size) for i in range(size)])  7.73 us
  transfers between devices with their start and end apart: 9, of which 1 were waited for; matrix products, arithmetic and copies ran while one was open for 0% of the time, Pallas kernels for 46%

profile of v2, /device:TPU:0, one launch (start us, length us, event | category | flops | bytes accessed | tf_op | source)
XLA Modules:
  0.0 47.0 jit_solution(5430931165513405720)
XLA Ops:
  0.6 1.0 %pack_coarse.1 = (f32[18,16,128]{2,1,0:T(8,128)S(1)}, f32[18,16,128]{2,1,0:T(8,128)S(1)}) custom-call(f32[4,16,16,128]{3,2,1,0:T(8,128)} %c0.4, f32[3,16,16,128]{3,2,1,0:T(8,128)} %cw.7), custom_call_target="tpu_custom_call" | custom-call | flops 1 | bytes 1 | tf_op jit(solution)/shard_map/pack_coarse/pallas_call | solution.py:568
  1.6 3.1 %collective-permute-start.6 = (f32[18,16,128]{2,1,0:T(8,128)S(1)}, f32[18,16,128]{2,1,0:T(8,128)S(1)}, u32[]{:S(2)}, u32[]{:S(2)}) collective-permute-start(f32[18,16,128]{2,1,0:T(8,128)S(1)} %get-tuple-element.160), channel_id=1, source_target_pairs={{0,8},{8,16},{16,24},{24,0},{1,9},{9,17},{17,25},{25,1},{2,10},{10... | collective-permute-start | bytes 442376 | tf_op jit(solution)/shard_map/ppermute | solution.py:582
  4.7 0.0 copy-start
  4.7 0.0 copy-start.1
  4.7 2.1 %collective-permute-start.7 = (f32[18,16,128]{2,1,0:T(8,128)S(1)}, f32[18,16,128]{2,1,0:T(8,128)S(1)}, u32[]{:S(2)}, u32[]{:S(2)}) collective-permute-start(f32[18,16,128]{2,1,0:T(8,128)S(1)} %get-tuple-element.161), channel_id=1, source_target_pairs={{0,24},{8,0},{16,8},{24,16},{1,25},{9,1},{17,9},{25,17},{2,26},{10... | collective-permute-start | bytes 442376 | tf_op jit(solution)/shard_map/ppermute | solution.py:582
  6.8 1.6 %pack_fine.1 = (f32[20,16,128]{2,1,0:T(8,128)}, f32[20,16,128]{2,1,0:T(8,128)S(1)}) custom-call(f32[4,32,16,128]{3,2,1,0:T(8,128)} %f0.1, f32[3,32,16,128]{3,2,1,0:T(8,128)} %fw.1), custom_call_target="tpu_custom_call" | custom-call | flops 1 | bytes 1 | tf_op jit(solution)/shard_map/pack_fine/pallas_call | solution.py:568
  9.1 0.1 collective-permute-start.10
  9.2 3.8 %collective-permute-start.11 = (f32[20,16,128]{2,1,0:T(8,128)S(1)}, f32[20,16,128]{2,1,0:T(8,128)}, u32[]{:S(2)}, u32[]{:S(2)}) collective-permute-start(f32[20,16,128]{2,1,0:T(8,128)S(1)} %get-tuple-element.167), channel_id=1, source_target_pairs={{0,24},{8,0},{16,8},{24,16},{1,25},{9,1},{17,9},{25,17},{2,26},{10... | collective-permute-start | bytes 491528 | tf_op jit(solution)/shard_map/ppermute | solution.py:582
  13.0 0.0 copy-done
  13.0 0.0 copy-done.1
  13.0 3.0 %inner.1 = (f32[304,128]{1,0:T(8,128)S(1)}, f32[4,2,16,128]{3,2,1,0:T(8,128)S(1)}) custom-call(f32[4,16,16,128]{3,2,1,0:T(8,128)S(1)} %copy-done, f32[3,16,16,128]{3,2,1,0:T(8,128)S(1)} %copy-done.1), custom_call_target="tpu_custom_call" | custom-call | flops 1 | bytes 1 | tf_op jit(solution)/shard_map/inner/pallas_call | solution.py:568
  16.1 0.0 collective-permute-done.6.lo
  16.1 0.0 collective-permute-done.7.hi
  16.1 0.8 %ypack.1 = (f32[318,128]{1,0:T(8,128)}, f32[318,128]{1,0:T(8,128)}) custom-call(f32[4,16,16,128]{3,2,1,0:T(8,128)S(1)} %copy-done, f32[3,16,16,128]{3,2,1,0:T(8,128)S(1)} %copy-done.1, f32[18,16,128]{2,1,0:T(8,128)S(1)} %collective-permute-done.6.lo, f32[18,16,128]{2,1,0:T(8,128)S(1)} %collective-permute-done.7.hi), custom_call_target="tpu_custom_call" | custom-call | flops 1 | bytes 1 | tf_op jit(solution)/shard_map/ypack/pallas_call | solution.py:568
  16.9 0.0 collective-permute-start.8
  16.9 1.7 %collective-permute-start.9 = (f32[318,128]{1,0:T(8,128)}, f32[318,128]{1,0:T(8,128)S(1)}, u32[]{:S(2)}, u32[]{:S(2)}) collective-permute-start(f32[318,128]{1,0:T(8,128)} %get-tuple-element.163), channel_id=1, source_target_pairs={{0,6},{2,0},{4,2},{6,4},{1,7},{3,1},{5,3},{7,5},{8,14},{10,8},{12,... | collective-permute-start | bytes 488456 | tf_op jit(solution)/shard_map/ppermute | solution.py:582
  18.7 1.7 %slab.1 = f32[304,128]{1,0:T(8,128)S(1)} custom-call(f32[4,16,16,128]{3,2,1,0:T(8,128)S(1)} %copy-done, f32[3,16,16,128]{3,2,1,0:T(8,128)S(1)} %copy-done.1, f32[18,16,128]{2,1,0:T(8,128)S(1)} %collective-permute-done.6.lo, f32[18,16,128]{2,1,0:T(8,128)S(1)} %collective-permute-done.7.hi, f32[304,128]{1,0:T(8,128)S(1)} %get-tuple-element.164.part, ...), custom_call_target="tpu_custom_call" | custom-call | flops 1 | bytes 1 | tf_op jit(solution)/shard_map/slab/pallas_call | solution.py:568
  20.4 0.0 copy-start.3
  20.4 7.8 %conditional.2 = (f32[304,128]{1,0:T(8,128)S(1)}) conditional(s32[]{:T(128)} %clamp.7, f32[304,128]{1,0:T(8,128)S(1)} %slab.1, f32[304,128]{1,0:T(8,128)S(1)} %slab.1, f32[304,128]{1,0:T(8,128)S(1)} %slab.1, f32[304,128]{1,0:T(8,128)S(1)} %slab.1), branch_computations={%region_0.1_spmd, %region_1.2_spmd, %region_2.3_spmd, %region_3.4_... | conditional | bytes 933936 | solution.py:593
  20.4 0.1 collective-permute-start
  20.5 7.7 %collective-permute-done = f32[304,128]{1,0:T(8,128)S(1)} collective-permute-done((f32[304,128]{1,0:T(8,128)S(1)}, f32[304,128]{1,0:T(8,128)S(1)}, u32[]{:S(2)}, u32[]{:S(2)}) %collective-permute-start) | collective-permute-done | bytes 155680 | tf_op jit(solution)/shard_map/cond/branch_1_fun/ppermute | solution.py:582
  28.2 0.0 copy-start.4
  28.2 0.7 %copy-done.4 = f32[304,128]{1,0:T(8,128)} copy-done((f32[304,128]{1,0:T(8,128)}, f32[304,128]{1,0:T(8,128)S(1)}, u32[]{:S(2)}) %copy-start.4) | copy-done | bytes 155672
  28.9 0.0 copy-start.2
  28.9 0.0 copy-start.5
  28.9 0.0 collective-permute-done.10.flo_there
  28.9 0.0 collective-permute-done.11.fhi_there
  28.9 0.0 collective-permute-done.8.below
  28.9 0.0 collective-permute-done.9.above
  28.9 0.5 %zpack.1 = f32[7,24,128]{2,1,0:T(8,128)S(1)} custom-call(f32[4,16,16,128]{3,2,1,0:T(8,128)S(1)} %copy-done, f32[3,16,16,128]{3,2,1,0:T(8,128)S(1)} %copy-done.1, f32[18,16,128]{2,1,0:T(8,128)S(1)} %collective-permute-done.6.lo, f32[18,16,128]{2,1,0:T(8,128)S(1)} %collective-permute-done.7.hi, f32[318,128]{1,0:T(8,128)S(1)} %collective-permute-done.8.below, ...), custom_call_target="tpu_custom_call" | custom-call | flops 1 | bytes 1 | tf_op jit(solution)/shard_map/zpack/pallas_call | solution.py:568
  29.5 0.9 %collective-permute-start.12 = (f32[7,24,128]{2,1,0:T(8,128)S(1)}, f32[7,24,128]{2,1,0:T(8,128)S(1)}, u32[]{:S(2)}, u32[]{:S(2)}) collective-permute-start(f32[7,24,128]{2,1,0:T(8,128)S(1)} %zpack.1), channel_id=1, source_target_pairs={{0,1},{1,0},{2,3},{3,2},{4,5},{5,4},{6,7},{7,6},{8,9},{9,8},{10,11... | collective-permute-start | bytes 258056 | tf_op jit(solution)/shard_map/ppermute | solution.py:604
  30.4 0.1 add_convert_fusion
  30.4 0.0 copy-done.3
  30.4 0.0 copy-done.2
  30.4 0.0 copy-done.5
  30.4 7.6 %fine.1 = (f32[4,32,16,128]{3,2,1,0:T(8,128)}, f32[4,8,8,128]{3,2,1,0:T(8,128)S(1)}) custom-call(f32[4,32,16,128]{3,2,1,0:T(8,128)S(1)} %copy-done.2, f32[3,32,16,128]{3,2,1,0:T(8,128)S(1)} %copy-done.3, f32[20,16,128]{2,1,0:T(8,128)} %collective-permute-done.10.flo_there, f32[20,16,128]{2,1,0:T(8,128)} %collective-permute-done.11.fhi_there, ...), custom_call_target="tpu_custom_call" | custom-call | flops 1 | bytes 1 | tf_op jit(solution)/shard_map/fine/pallas_call | solution.py:568
  38.1 0.0 collective-permute-done.12
  38.1 8.0 %conditional.3 = (f32[4,8,8,128]{3,2,1,0:T(8,128)S(1)}, f32[4,16,16,128]{3,2,1,0:T(8,128)S(1)}) conditional(s32[]{:T(128)} %clamp.6, (s32[1,2]{1,0:T(1,128)S(1)}, f32[4,16,16,128]{3,2,1,0:T(8,128)S(1)}, f32[3,16,16,128]{3,2,1,0:T(8,128)S(1)}, f32[18,16,128]{2,1,0:T(8,128)S(1)}, f32[18,16,128]{2,1,0:T(8,128)S(1)}, ...), branch_computations={%region_4.5_spmd, %region_5.6_spmd, %region_6.7_spmd, %region_7.8_... | conditional | flops 40000000 | bytes 4786488 | solution.py:593
  38.1 1.0 %collective-permute-start.5 = (f32[4,8,8,128]{3,2,1,0:T(8,128)S(1)}, f32[4,8,8,128]{3,2,1,0:T(8,128)S(1)}, u32[]{:S(2)}, u32[]{:S(2)}) collective-permute-start(f32[4,8,8,128]{3,2,1,0:T(8,128)S(1)} %get-tuple-element.119), channel_id=1, source_target_pairs={{0,24},{8,0},{16,8},{24,16},{1,25},{9,1},{17,9},{25,17},{2,26},{10... | collective-permute-start | bytes 393224 | tf_op jit(solution)/shard_map/cond/branch_3_fun/ppermute | solution.py:582
  39.2 6.9 %coarse.7 = f32[4,16,16,128]{3,2,1,0:T(8,128)S(1)} custom-call(s32[1,2]{1,0:T(1,128)S(1)} %get-tuple-element.120.sides, f32[4,16,16,128]{3,2,1,0:T(8,128)S(1)} %get-tuple-element.121.c0, f32[3,16,16,128]{3,2,1,0:T(8,128)S(1)} %get-tuple-element.122.cw, f32[18,16,128]{2,1,0:T(8,128)S(1)} %get-tuple-element.123.lo, f32[18,16,128]{2,1,0:T(8,128)S(1)} %get-tuple-element.124.hi, ...), custom_call_target="tpu_custom_call" | custom-call | flops 40000000 | bytes 4000000 | tf_op jit(solution)/shard_map/cond/branch_3_fun/coarse/pallas_call | solution.py:568
  46.1 0.0 collective-permute-done.5
  46.1 0.9 %merge.1 = f32[4,16,16,128]{3,2,1,0:T(8,128)} custom-call(f32[4,16,16,128]{3,2,1,0:T(8,128)S(1)} %get-tuple-element.174.c3, f32[4,8,8,128]{3,2,1,0:T(8,128)S(1)} %get-tuple-element.175.avg), custom_call_target="tpu_custom_call" | custom-call | flops 1 | bytes 1 | tf_op jit(solution)/shard_map/merge/pallas_call | solution.py:568
  (2 shorter events, 0.0 us)
Async XLA Ops:
  1.6 14.4 %collective-permute-start.6 = (f32[18,16,128]{2,1,0:T(8,128)S(1)}, f32[18,16,128]{2,1,0:T(8,128)S(1)}, u32[]{:S(2)}, u32[]{:S(2)}) collective-permute-start(f32[18,16,128]{2,1,0:T(8,128)S(1)} %get-tuple-element.160), channel_id=1, source_target_pairs={{0,8},{8,16},{16,24},{24,0},{1,9},{9,17},{17,25},{25,1},{2,10},{10... | collective-permute-start | bytes 442376 | tf_op jit(solution)/shard_map/ppermute | solution.py:582
  4.7 8.3 %copy-start = (f32[4,16,16,128]{3,2,1,0:T(8,128)S(1)}, f32[4,16,16,128]{3,2,1,0:T(8,128)}, u32[]{:S(2)}) copy-start(f32[4,16,16,128]{3,2,1,0:T(8,128)} %c0.4) | copy-start | bytes 1572868
  4.7 8.3 %copy-start.1 = (f32[3,16,16,128]{3,2,1,0:T(8,128)S(1)}, f32[3,16,16,128]{3,2,1,0:T(8,128)}, u32[]{:S(2)}) copy-start(f32[3,16,16,128]{3,2,1,0:T(8,128)} %cw.7) | copy-start | bytes 1179652
  4.7 11.4 %collective-permute-start.7 = (f32[18,16,128]{2,1,0:T(8,128)S(1)}, f32[18,16,128]{2,1,0:T(8,128)S(1)}, u32[]{:S(2)}, u32[]{:S(2)}) collective-permute-start(f32[18,16,128]{2,1,0:T(8,128)S(1)} %get-tuple-element.161), channel_id=1, source_target_pairs={{0,24},{8,0},{16,8},{24,16},{1,25},{9,1},{17,9},{25,17},{2,26},{10... | collective-permute-start | bytes 442376 | tf_op jit(solution)/shard_map/ppermute | solution.py:582
  9.1 19.8 %collective-permute-start.10 = (f32[20,16,128]{2,1,0:T(8,128)}, f32[20,16,128]{2,1,0:T(8,128)}, u32[]{:S(2)}, u32[]{:S(2)}) collective-permute-start(f32[20,16,128]{2,1,0:T(8,128)} %get-tuple-element.166), channel_id=1, source_target_pairs={{0,8},{8,16},{16,24},{24,0},{1,9},{9,17},{17,25},{25,1},{2,10},{10... | collective-permute-start | bytes 491528 | tf_op jit(solution)/shard_map/ppermute | solution.py:582
  9.2 19.7 %collective-permute-start.11 = (f32[20,16,128]{2,1,0:T(8,128)S(1)}, f32[20,16,128]{2,1,0:T(8,128)}, u32[]{:S(2)}, u32[]{:S(2)}) collective-permute-start(f32[20,16,128]{2,1,0:T(8,128)S(1)} %get-tuple-element.167), channel_id=1, source_target_pairs={{0,24},{8,0},{16,8},{24,16},{1,25},{9,1},{17,9},{25,17},{2,26},{10... | collective-permute-start | bytes 491528 | tf_op jit(solution)/shard_map/ppermute | solution.py:582
  16.9 12.0 %collective-permute-start.8 = (f32[318,128]{1,0:T(8,128)}, f32[318,128]{1,0:T(8,128)S(1)}, u32[]{:S(2)}, u32[]{:S(2)}) collective-permute-start(f32[318,128]{1,0:T(8,128)} %get-tuple-element.162), channel_id=1, source_target_pairs={{0,2},{2,4},{4,6},{6,0},{1,3},{3,5},{5,7},{7,1},{8,10},{10,12},{12... | collective-permute-start | bytes 488456 | tf_op jit(solution)/shard_map/ppermute | solution.py:582
  16.9 12.0 %collective-permute-start.9 = (f32[318,128]{1,0:T(8,128)}, f32[318,128]{1,0:T(8,128)S(1)}, u32[]{:S(2)}, u32[]{:S(2)}) collective-permute-start(f32[318,128]{1,0:T(8,128)} %get-tuple-element.163), channel_id=1, source_target_pairs={{0,6},{2,0},{4,2},{6,4},{1,7},{3,1},{5,3},{7,5},{8,14},{10,8},{12,... | collective-permute-start | bytes 488456 | tf_op jit(solution)/shard_map/ppermute | solution.py:582
  20.4 10.0 %copy-start.3 = (f32[3,32,16,128]{3,2,1,0:T(8,128)S(1)}, f32[3,32,16,128]{3,2,1,0:T(8,128)}, u32[]{:S(2)}) copy-start(f32[3,32,16,128]{3,2,1,0:T(8,128)} %fw.1) | copy-start | bytes 2359300
  20.4 7.8 %collective-permute-start = (f32[304,128]{1,0:T(8,128)S(1)}, f32[304,128]{1,0:T(8,128)S(1)}, u32[]{:S(2)}, u32[]{:S(2)}) collective-permute-start(f32[304,128]{1,0:T(8,128)S(1)} %param.1), channel_id=1, source_target_pairs={{0,8},{8,16},{16,24},{24,0},{1,9},{9,17},{17,25},{25,1},{2,10},{10... | collective-permute-start | bytes 466952 | tf_op jit(solution)/shard_map/cond/branch_1_fun/ppermute | solution.py:582
  28.2 0.7 %copy-start.4 = (f32[304,128]{1,0:T(8,128)}, f32[304,128]{1,0:T(8,128)S(1)}, u32[]{:S(2)}) copy-start(f32[304,128]{1,0:T(8,128)S(1)} %get-tuple-element.185.slab) | copy-start | bytes 466948
  28.9 1.5 %copy-start.2 = (f32[4,32,16,128]{3,2,1,0:T(8,128)S(1)}, f32[4,32,16,128]{3,2,1,0:T(8,128)}, u32[]{:S(2)}) copy-start(f32[4,32,16,128]{3,2,1,0:T(8,128)} %f0.1) | copy-start | bytes 3145732
  28.9 1.5 %copy-start.5 = (f32[304,128]{1,0:T(8,128)S(1)}, f32[304,128]{1,0:T(8,128)}, u32[]{:S(2)}) copy-start(f32[304,128]{1,0:T(8,128)} %copy-done.4) | copy-start | bytes 466948
  29.5 8.6 %collective-permute-start.12 = (f32[7,24,128]{2,1,0:T(8,128)S(1)}, f32[7,24,128]{2,1,0:T(8,128)S(1)}, u32[]{:S(2)}, u32[]{:S(2)}) collective-permute-start(f32[7,24,128]{2,1,0:T(8,128)S(1)} %zpack.1), channel_id=1, source_target_pairs={{0,1},{1,0},{2,3},{3,2},{4,5},{5,4},{6,7},{7,6},{8,9},{9,8},{10,11... | collective-permute-start | bytes 258056 | tf_op jit(solution)/shard_map/ppermute | solution.py:604
  38.1 7.9 %collective-permute-start.5 = (f32[4,8,8,128]{3,2,1,0:T(8,128)S(1)}, f32[4,8,8,128]{3,2,1,0:T(8,128)S(1)}, u32[]{:S(2)}, u32[]{:S(2)}) collective-permute-start(f32[4,8,8,128]{3,2,1,0:T(8,128)S(1)} %get-tuple-element.119), channel_id=1, source_target_pairs={{0,24},{8,0},{16,8},{24,16},{1,25},{9,1},{17,9},{25,17},{2,26},{10... | collective-permute-start | bytes 393224 | tf_op jit(solution)/shard_map/cond/branch_3_fun/ppermute | solution.py:582

commit v3 on v2

--- a/solution.py
+++ b/solution.py
@@ -188,12 +188,15 @@
 
         def layer(j, carry, step=step, src=src, dst=dst):
             w = coefficients(section_weights[step], [cw[d, j] for d in range(3)])
+            made = []
             for f in range(q):
                 base = None if step == 0 else c0[f, j]
-                dst[f, j] = turned(base, section_weights[step], w, src[f, j], src[f, j - 1], src[f, j + 1])
+                made.append(turned(base, section_weights[step], w, src[f, j], src[f, j - 1], src[f, j + 1]))
+            for f in range(q):
+                dst[f, j] = made[f]
             return carry
 
-        unrolled(step + 1, x - 1 - step, 2, layer)
+        unrolled(step + 1, x - 1 - step, 7 if step == 0 else 6, layer)
     for f in range(q):
         near[f, 0] = state1[f, EDGE - 2]
         near[f, 1] = state1[f, x + 1 - EDGE]
@@ -331,6 +334,7 @@
         def two_layers(t, packed, step=step, src=src, flat=flat, fraction=fraction, skip=skip, height=height):
             first = step + 2 * t
             packed = list(packed)
+            made = []
             co = []
             for a in (first, first + 1):
                 if step < 2:
@@ -364,13 +368,15 @@
                         pltpu.roll(jnp.where(is_last, ghost, center), 1, 1),
                         pltpu.roll(jnp.where(is_first, ghost, center), z - 1, 1),
                     )
-                    if step == 2:
-                        out[f, a - 2] = value
-                    else:
-                        pads[step + 1][f, a + 1, BLOCK, :] = value
+                    made.append((f, a, value))
                     if step == 0:
                         ends = jnp.where(is_first | is_last, value, 0.0)
                         packed[f] = packed[f] + pltpu.roll(ends, 6 * a + 3, 1)
+            for f, a, value in made:
+                if step == 2:
+                    out[f, a - 2] = value
+                else:
+                    pads[step + 1][f, a + 1, BLOCK, :] = value
             return tuple(packed)
 
         start = tuple(jnp.zeros((24, z), F32) for _ in range(q)) if step == 0 else ()
@@ -468,6 +474,7 @@
             else:
                 winds = [layer_of(s, fw, flo, fhi, d, at, 2, 3 * q) for d in range(3)]
             co.append(coefficients(fraction, winds))
+        made = []
         for f in range(q):
             if k == 0:
                 row_of = [field(f, 2 * t - 3 + i) for i in range(4)]
@@ -490,7 +497,7 @@
                     y_low, y_high = flat[pl.ds(row - 1, y), :], flat[pl.ds(row + 1, y), :]
                 ghost = zface[(odd * q + f) * y : (odd * q + f + 1) * y, :]
                 ghost = pltpu.roll(ghost, (2 * z - 2 * s.ex * k - 2 * t) if inner else -(2 * s.ex * k + 2 * t) % z, 1)
-                states[k + 1][f, b + 1, rows, :] = advanced(
+                value = advanced(
                     None if k == 0 else field(f, b - 2),
                     fraction,
                     co[odd],
@@ -502,6 +509,9 @@
                     pltpu.roll(jnp.where(is_last, ghost, center), 1, 1),
                     pltpu.roll(jnp.where(is_first, ghost, center), z - 1, 1),
                 )
+                made.append((f, b, value))
+        for f, b, value in made:
+            states[k + 1][f, b + 1, rows, :] = value
 
     for move in arrivals:
         move.wait()

time: 47.1 us -> 46.4 us (0.985)
  Pallas kernels: 24.2 us -> 23.6 us
    ppermute x1, starting transfers between devices: 0.9 us -> 0.21 us  [z_columns(): return lax.ppermute(zown, 'gz', [(0, 1), (1, 0)])]
    pallas_call x9, Pallas kernels: 24.2 us -> 23.6 us  [run(): pl.pallas_call(kernel, out_shape=tuple((space(dims, F32) for dims, space...]
where the time goes in v3:
time: 46.4 us; the launch traced here: 46.6 us
  Pallas kernels  23.6 us (51%)
  starting transfers between devices  12.5 us (27%)
  waiting for transfers between devices  7.73 us (17%)
  between operations  1.43 us (3%)
  local copies, waits for them, and re-layouts  1.08 us (2%)
    pallas_call x9, Pallas kernels, run(): pl.pallas_call(kernel, out_shape=tuple((space(dims, F32) for dims, space...  23.6 us
    ppermute x8, starting transfers between devices, ring(): lax.ppermute(array, axis, [(i, (i + by) % size) for i in range(size)])  12.3 us
    ppermute x8, waiting for transfers between devices, ring(): lax.ppermute(array, axis, [(i, (i + by) % size) for i in range(size)])  7.73 us
    unnamed x12, local copies, waits for them, and re-layouts  1.06 us
  transfers between devices with their start and end apart: 9, of which 1 were waited for; matrix products, arithmetic and copies ran while one was open for 0% of the time, Pallas kernels for 46%

profile of v3, /device:TPU:0, one launch (start us, length us, event | category | flops | bytes accessed | tf_op | source)
XLA Modules:
  0.0 46.6 jit_solution(1154149524906913221)
XLA Ops:
  0.6 1.0 %pack_coarse.1 = (f32[18,16,128]{2,1,0:T(8,128)S(1)}, f32[18,16,128]{2,1,0:T(8,128)S(1)}) custom-call(f32[4,16,16,128]{3,2,1,0:T(8,128)} %c0.4, f32[3,16,16,128]{3,2,1,0:T(8,128)} %cw.7), custom_call_target="tpu_custom_call" | custom-call | flops 1 | bytes 1 | tf_op jit(solution)/shard_map/pack_coarse/pallas_call | solution.py:578
  1.6 3.1 %collective-permute-start.6 = (f32[18,16,128]{2,1,0:T(8,128)S(1)}, f32[18,16,128]{2,1,0:T(8,128)S(1)}, u32[]{:S(2)}, u32[]{:S(2)}) collective-permute-start(f32[18,16,128]{2,1,0:T(8,128)S(1)} %get-tuple-element.160), channel_id=1, source_target_pairs={{0,8},{8,16},{16,24},{24,0},{1,9},{9,17},{17,25},{25,1},{2,10},{10... | collective-permute-start | bytes 442376 | tf_op jit(solution)/shard_map/ppermute | solution.py:592
  4.7 0.0 copy-start
  4.7 0.0 copy-start.1
  4.7 2.1 %collective-permute-start.7 = (f32[18,16,128]{2,1,0:T(8,128)S(1)}, f32[18,16,128]{2,1,0:T(8,128)S(1)}, u32[]{:S(2)}, u32[]{:S(2)}) collective-permute-start(f32[18,16,128]{2,1,0:T(8,128)S(1)} %get-tuple-element.161), channel_id=1, source_target_pairs={{0,24},{8,0},{16,8},{24,16},{1,25},{9,1},{17,9},{25,17},{2,26},{10... | collective-permute-start | bytes 442376 | tf_op jit(solution)/shard_map/ppermute | solution.py:592
  6.8 1.6 %pack_fine.1 = (f32[20,16,128]{2,1,0:T(8,128)}, f32[20,16,128]{2,1,0:T(8,128)S(1)}) custom-call(f32[4,32,16,128]{3,2,1,0:T(8,128)} %f0.1, f32[3,32,16,128]{3,2,1,0:T(8,128)} %fw.1), custom_call_target="tpu_custom_call" | custom-call | flops 1 | bytes 1 | tf_op jit(solution)/shard_map/pack_fine/pallas_call | solution.py:578
  9.1 0.1 collective-permute-start.10
  9.2 3.8 %collective-permute-start.11 = (f32[20,16,128]{2,1,0:T(8,128)S(1)}, f32[20,16,128]{2,1,0:T(8,128)}, u32[]{:S(2)}, u32[]{:S(2)}) collective-permute-start(f32[20,16,128]{2,1,0:T(8,128)S(1)} %get-tuple-element.167), channel_id=1, source_target_pairs={{0,24},{8,0},{16,8},{24,16},{1,25},{9,1},{17,9},{25,17},{2,26},{10... | collective-permute-start | bytes 491528 | tf_op jit(solution)/shard_map/ppermute | solution.py:592
  13.0 0.0 copy-done
  13.0 0.0 copy-done.1
  13.0 2.5 %inner.1 = (f32[304,128]{1,0:T(8,128)S(1)}, f32[4,2,16,128]{3,2,1,0:T(8,128)S(1)}) custom-call(f32[4,16,16,128]{3,2,1,0:T(8,128)S(1)} %copy-done, f32[3,16,16,128]{3,2,1,0:T(8,128)S(1)} %copy-done.1), custom_call_target="tpu_custom_call" | custom-call | flops 1 | bytes 1 | tf_op jit(solution)/shard_map/inner/pallas_call | solution.py:578
  15.5 0.0 collective-permute-done.6.lo
  15.5 0.0 collective-permute-done.7.hi
  15.5 0.8 %ypack.1 = (f32[318,128]{1,0:T(8,128)}, f32[318,128]{1,0:T(8,128)}) custom-call(f32[4,16,16,128]{3,2,1,0:T(8,128)S(1)} %copy-done, f32[3,16,16,128]{3,2,1,0:T(8,128)S(1)} %copy-done.1, f32[18,16,128]{2,1,0:T(8,128)S(1)} %collective-permute-done.6.lo, f32[18,16,128]{2,1,0:T(8,128)S(1)} %collective-permute-done.7.hi), custom_call_target="tpu_custom_call" | custom-call | flops 1 | bytes 1 | tf_op jit(solution)/shard_map/ypack/pallas_call | solution.py:578
  16.3 0.0 collective-permute-start.8
  16.4 1.7 %collective-permute-start.9 = (f32[318,128]{1,0:T(8,128)}, f32[318,128]{1,0:T(8,128)S(1)}, u32[]{:S(2)}, u32[]{:S(2)}) collective-permute-start(f32[318,128]{1,0:T(8,128)} %get-tuple-element.163), channel_id=1, source_target_pairs={{0,6},{2,0},{4,2},{6,4},{1,7},{3,1},{5,3},{7,5},{8,14},{10,8},{12,... | collective-permute-start | bytes 488456 | tf_op jit(solution)/shard_map/ppermute | solution.py:592
  18.1 1.7 %slab.1 = f32[304,128]{1,0:T(8,128)S(1)} custom-call(f32[4,16,16,128]{3,2,1,0:T(8,128)S(1)} %copy-done, f32[3,16,16,128]{3,2,1,0:T(8,128)S(1)} %copy-done.1, f32[18,16,128]{2,1,0:T(8,128)S(1)} %collective-permute-done.6.lo, f32[18,16,128]{2,1,0:T(8,128)S(1)} %collective-permute-done.7.hi, f32[304,128]{1,0:T(8,128)S(1)} %get-tuple-element.164.part, ...), custom_call_target="tpu_custom_call" | custom-call | flops 1 | bytes 1 | tf_op jit(solution)/shard_map/slab/pallas_call | solution.py:578
  19.8 0.0 copy-start.3
  19.8 7.8 %conditional.2 = (f32[304,128]{1,0:T(8,128)S(1)}) conditional(s32[]{:T(128)} %clamp.7, f32[304,128]{1,0:T(8,128)S(1)} %slab.1, f32[304,128]{1,0:T(8,128)S(1)} %slab.1, f32[304,128]{1,0:T(8,128)S(1)} %slab.1, f32[304,128]{1,0:T(8,128)S(1)} %slab.1), branch_computations={%region_0.1_spmd, %region_1.2_spmd, %region_2.3_spmd, %region_3.4_... | conditional | bytes 933936 | solution.py:603
  19.8 0.1 collective-permute-start
  19.9 7.7 %collective-permute-done = f32[304,128]{1,0:T(8,128)S(1)} collective-permute-done((f32[304,128]{1,0:T(8,128)S(1)}, f32[304,128]{1,0:T(8,128)S(1)}, u32[]{:S(2)}, u32[]{:S(2)}) %collective-permute-start) | collective-permute-done | bytes 155680 | tf_op jit(solution)/shard_map/cond/branch_1_fun/ppermute | solution.py:592
  27.7 0.0 copy-start.4
  27.7 0.7 %copy-done.4 = f32[304,128]{1,0:T(8,128)} copy-done((f32[304,128]{1,0:T(8,128)}, f32[304,128]{1,0:T(8,128)S(1)}, u32[]{:S(2)}) %copy-start.4) | copy-done | bytes 155672
  28.3 0.0 copy-start.2
  28.3 0.0 copy-start.5
  28.3 0.0 collective-permute-done.10.flo_there
  28.3 0.0 collective-permute-done.11.fhi_there
  28.3 0.0 collective-permute-done.8.below
  28.3 0.0 collective-permute-done.9.above
  28.4 0.5 %zpack.1 = f32[7,24,128]{2,1,0:T(8,128)S(1)} custom-call(f32[4,16,16,128]{3,2,1,0:T(8,128)S(1)} %copy-done, f32[3,16,16,128]{3,2,1,0:T(8,128)S(1)} %copy-done.1, f32[18,16,128]{2,1,0:T(8,128)S(1)} %collective-permute-done.6.lo, f32[18,16,128]{2,1,0:T(8,128)S(1)} %collective-permute-done.7.hi, f32[318,128]{1,0:T(8,128)S(1)} %collective-permute-done.8.below, ...), custom_call_target="tpu_custom_call" | custom-call | flops 1 | bytes 1 | tf_op jit(solution)/shard_map/zpack/pallas_call | solution.py:578
  28.9 0.2 collective-permute-start.12
  29.1 0.1 add_convert_fusion
  29.2 0.0 copy-done.3
  29.2 0.4 copy-done.2
  29.6 0.0 copy-done.5
  29.6 7.6 %fine.1 = (f32[4,32,16,128]{3,2,1,0:T(8,128)}, f32[4,8,8,128]{3,2,1,0:T(8,128)S(1)}) custom-call(f32[4,32,16,128]{3,2,1,0:T(8,128)S(1)} %copy-done.2, f32[3,32,16,128]{3,2,1,0:T(8,128)S(1)} %copy-done.3, f32[20,16,128]{2,1,0:T(8,128)} %collective-permute-done.10.flo_there, f32[20,16,128]{2,1,0:T(8,128)} %collective-permute-done.11.fhi_there, ...), custom_call_target="tpu_custom_call" | custom-call | flops 1 | bytes 1 | tf_op jit(solution)/shard_map/fine/pallas_call | solution.py:578
  37.2 0.0 collective-permute-done.12
  37.2 8.4 %conditional.3 = (f32[4,8,8,128]{3,2,1,0:T(8,128)S(1)}, f32[4,16,16,128]{3,2,1,0:T(8,128)S(1)}) conditional(s32[]{:T(128)} %clamp.6, (s32[1,2]{1,0:T(1,128)S(1)}, f32[4,16,16,128]{3,2,1,0:T(8,128)S(1)}, f32[3,16,16,128]{3,2,1,0:T(8,128)S(1)}, f32[18,16,128]{2,1,0:T(8,128)S(1)}, f32[18,16,128]{2,1,0:T(8,128)S(1)}, ...), branch_computations={%region_4.5_spmd, %region_5.6_spmd, %region_6.7_spmd, %region_7.8_... | conditional | flops 40000000 | bytes 4786488 | solution.py:603
  37.3 1.4 %collective-permute-start.5 = (f32[4,8,8,128]{3,2,1,0:T(8,128)S(1)}, f32[4,8,8,128]{3,2,1,0:T(8,128)S(1)}, u32[]{:S(2)}, u32[]{:S(2)}) collective-permute-start(f32[4,8,8,128]{3,2,1,0:T(8,128)S(1)} %get-tuple-element.119), channel_id=1, source_target_pairs={{0,24},{8,0},{16,8},{24,16},{1,25},{9,1},{17,9},{25,17},{2,26},{10... | collective-permute-start | bytes 393224 | tf_op jit(solution)/shard_map/cond/branch_3_fun/ppermute | solution.py:592
  38.7 6.9 %coarse.7 = f32[4,16,16,128]{3,2,1,0:T(8,128)S(1)} custom-call(s32[1,2]{1,0:T(1,128)S(1)} %get-tuple-element.120.sides, f32[4,16,16,128]{3,2,1,0:T(8,128)S(1)} %get-tuple-element.121.c0, f32[3,16,16,128]{3,2,1,0:T(8,128)S(1)} %get-tuple-element.122.cw, f32[18,16,128]{2,1,0:T(8,128)S(1)} %get-tuple-element.123.lo, f32[18,16,128]{2,1,0:T(8,128)S(1)} %get-tuple-element.124.hi, ...), custom_call_target="tpu_custom_call" | custom-call | flops 40000000 | bytes 4000000 | tf_op jit(solution)/shard_map/cond/branch_3_fun/coarse/pallas_call | solution.py:578
  45.6 0.0 collective-permute-done.5
  45.6 0.9 %merge.1 = f32[4,16,16,128]{3,2,1,0:T(8,128)} custom-call(f32[4,16,16,128]{3,2,1,0:T(8,128)S(1)} %get-tuple-element.174.c3, f32[4,8,8,128]{3,2,1,0:T(8,128)S(1)} %get-tuple-element.175.avg), custom_call_target="tpu_custom_call" | custom-call | flops 1 | bytes 1 | tf_op jit(solution)/shard_map/merge/pallas_call | solution.py:578
  (2 shorter events, 0.0 us)
Async XLA Ops:
  1.6 13.9 %collective-permute-start.6 = (f32[18,16,128]{2,1,0:T(8,128)S(1)}, f32[18,16,128]{2,1,0:T(8,128)S(1)}, u32[]{:S(2)}, u32[]{:S(2)}) collective-permute-start(f32[18,16,128]{2,1,0:T(8,128)S(1)} %get-tuple-element.160), channel_id=1, source_target_pairs={{0,8},{8,16},{16,24},{24,0},{1,9},{9,17},{17,25},{25,1},{2,10},{10... | collective-permute-start | bytes 442376 | tf_op jit(solution)/shard_map/ppermute | solution.py:592
  4.7 8.3 %copy-start = (f32[4,16,16,128]{3,2,1,0:T(8,128)S(1)}, f32[4,16,16,128]{3,2,1,0:T(8,128)}, u32[]{:S(2)}) copy-start(f32[4,16,16,128]{3,2,1,0:T(8,128)} %c0.4) | copy-start | bytes 1572868
  4.7 8.3 %copy-start.1 = (f32[3,16,16,128]{3,2,1,0:T(8,128)S(1)}, f32[3,16,16,128]{3,2,1,0:T(8,128)}, u32[]{:S(2)}) copy-start(f32[3,16,16,128]{3,2,1,0:T(8,128)} %cw.7) | copy-start | bytes 1179652
  4.7 10.8 %collective-permute-start.7 = (f32[18,16,128]{2,1,0:T(8,128)S(1)}, f32[18,16,128]{2,1,0:T(8,128)S(1)}, u32[]{:S(2)}, u32[]{:S(2)}) collective-permute-start(f32[18,16,128]{2,1,0:T(8,128)S(1)} %get-tuple-element.161), channel_id=1, source_target_pairs={{0,24},{8,0},{16,8},{24,16},{1,25},{9,1},{17,9},{25,17},{2,26},{10... | collective-permute-start | bytes 442376 | tf_op jit(solution)/shard_map/ppermute | solution.py:592
  9.1 19.2 %collective-permute-start.10 = (f32[20,16,128]{2,1,0:T(8,128)}, f32[20,16,128]{2,1,0:T(8,128)}, u32[]{:S(2)}, u32[]{:S(2)}) collective-permute-start(f32[20,16,128]{2,1,0:T(8,128)} %get-tuple-element.166), channel_id=1, source_target_pairs={{0,8},{8,16},{16,24},{24,0},{1,9},{9,17},{17,25},{25,1},{2,10},{10... | collective-permute-start | bytes 491528 | tf_op jit(solution)/shard_map/ppermute | solution.py:592
  9.2 19.1 %collective-permute-start.11 = (f32[20,16,128]{2,1,0:T(8,128)S(1)}, f32[20,16,128]{2,1,0:T(8,128)}, u32[]{:S(2)}, u32[]{:S(2)}) collective-permute-start(f32[20,16,128]{2,1,0:T(8,128)S(1)} %get-tuple-element.167), channel_id=1, source_target_pairs={{0,24},{8,0},{16,8},{24,16},{1,25},{9,1},{17,9},{25,17},{2,26},{10... | collective-permute-start | bytes 491528 | tf_op jit(solution)/shard_map/ppermute | solution.py:592
  16.3 12.0 %collective-permute-start.8 = (f32[318,128]{1,0:T(8,128)}, f32[318,128]{1,0:T(8,128)S(1)}, u32[]{:S(2)}, u32[]{:S(2)}) collective-permute-start(f32[318,128]{1,0:T(8,128)} %get-tuple-element.162), channel_id=1, source_target_pairs={{0,2},{2,4},{4,6},{6,0},{1,3},{3,5},{5,7},{7,1},{8,10},{10,12},{12... | collective-permute-start | bytes 488456 | tf_op jit(solution)/shard_map/ppermute | solution.py:592
  16.4 12.0 %collective-permute-start.9 = (f32[318,128]{1,0:T(8,128)}, f32[318,128]{1,0:T(8,128)S(1)}, u32[]{:S(2)}, u32[]{:S(2)}) collective-permute-start(f32[318,128]{1,0:T(8,128)} %get-tuple-element.163), channel_id=1, source_target_pairs={{0,6},{2,0},{4,2},{6,4},{1,7},{3,1},{5,3},{7,5},{8,14},{10,8},{12,... | collective-permute-start | bytes 488456 | tf_op jit(solution)/shard_map/ppermute | solution.py:592
  19.8 9.4 %copy-start.3 = (f32[3,32,16,128]{3,2,1,0:T(8,128)S(1)}, f32[3,32,16,128]{3,2,1,0:T(8,128)}, u32[]{:S(2)}) copy-start(f32[3,32,16,128]{3,2,1,0:T(8,128)} %fw.1) | copy-start | bytes 2359300
  19.8 7.8 %collective-permute-start = (f32[304,128]{1,0:T(8,128)S(1)}, f32[304,128]{1,0:T(8,128)S(1)}, u32[]{:S(2)}, u32[]{:S(2)}) collective-permute-start(f32[304,128]{1,0:T(8,128)S(1)} %param.1), channel_id=1, source_target_pairs={{0,8},{8,16},{16,24},{24,0},{1,9},{9,17},{17,25},{25,1},{2,10},{10... | collective-permute-start | bytes 466952 | tf_op jit(solution)/shard_map/cond/branch_1_fun/ppermute | solution.py:592
  27.7 0.7 %copy-start.4 = (f32[304,128]{1,0:T(8,128)}, f32[304,128]{1,0:T(8,128)S(1)}, u32[]{:S(2)}) copy-start(f32[304,128]{1,0:T(8,128)S(1)} %get-tuple-element.185.slab) | copy-start | bytes 466948
  28.3 1.2 %copy-start.2 = (f32[4,32,16,128]{3,2,1,0:T(8,128)S(1)}, f32[4,32,16,128]{3,2,1,0:T(8,128)}, u32[]{:S(2)}) copy-start(f32[4,32,16,128]{3,2,1,0:T(8,128)} %f0.1) | copy-start | bytes 3145732
  28.3 1.2 %copy-start.5 = (f32[304,128]{1,0:T(8,128)S(1)}, f32[304,128]{1,0:T(8,128)}, u32[]{:S(2)}) copy-start(f32[304,128]{1,0:T(8,128)} %copy-done.4) | copy-start | bytes 466948
  28.9 8.3 %collective-permute-start.12 = (f32[7,24,128]{2,1,0:T(8,128)S(1)}, f32[7,24,128]{2,1,0:T(8,128)S(1)}, u32[]{:S(2)}, u32[]{:S(2)}) collective-permute-start(f32[7,24,128]{2,1,0:T(8,128)S(1)} %zpack.1), channel_id=1, source_target_pairs={{0,1},{1,0},{2,3},{3,2},{4,5},{5,4},{6,7},{7,6},{8,9},{9,8},{10,11... | collective-permute-start | bytes 258056 | tf_op jit(solution)/shard_map/ppermute | solution.py:614
  37.3 8.4 %collective-permute-start.5 = (f32[4,8,8,128]{3,2,1,0:T(8,128)S(1)}, f32[4,8,8,128]{3,2,1,0:T(8,128)S(1)}, u32[]{:S(2)}, u32[]{:S(2)}) collective-permute-start(f32[4,8,8,128]{3,2,1,0:T(8,128)S(1)} %get-tuple-element.119), channel_id=1, source_target_pairs={{0,24},{8,0},{16,8},{24,16},{1,25},{9,1},{17,9},{25,17},{2,26},{10... | collective-permute-start | bytes 393224 | tf_op jit(solution)/shard_map/cond/branch_3_fun/ppermute | solution.py:592

commit v4 on v3

--- a/solution.py
+++ b/solution.py
@@ -333,7 +333,7 @@
 
         def two_layers(t, packed, step=step, src=src, flat=flat, fraction=fraction, skip=skip, height=height):
             first = step + 2 * t
-            packed = list(packed)
+            ghosts, packed = (list(some) for some in packed)
             made = []
             co = []
             for a in (first, first + 1):
@@ -350,12 +350,12 @@
                     row = (f * s.ep + layer) * WPAD + 8 + skip + by
                     return of.reshape(flat.shape)[pl.ds(row, height), :]
 
-                beside = flat_beyond[pl.ds((step * q + f) * 24 + skip, height), :]
                 row_of = [at_layer(src, first + i) for i in range(4)]
                 for i in range(2):
                     a = first + i
                     center = row_of[i + 1]
-                    ghost = pltpu.roll(beside, 2 * z - 6 * a - 3, 1)
+                    ghost = ghosts[f]
+                    ghosts[f] = pltpu.roll(ghost, z - 6, 1)
                     value = advanced(
                         None if step == 0 else at_layer(pad0, a + 1),
                         fraction,
@@ -370,22 +370,25 @@
                     )
                     made.append((f, a, value))
                     if step == 0:
-                        ends = jnp.where(is_first | is_last, value, 0.0)
-                        packed[f] = packed[f] + pltpu.roll(ends, 6 * a + 3, 1)
+                        packed[f] = pltpu.roll(packed[f] + jnp.where(is_first | is_last, value, 0.0), z - 6, 1)
             for f, a, value in made:
                 if step == 2:
                     out[f, a - 2] = value
                 else:
                     pads[step + 1][f, a + 1, BLOCK, :] = value
-            return tuple(packed)
-
-        start = tuple(jnp.zeros((24, z), F32) for _ in range(q)) if step == 0 else ()
-        packed = unrolled(0, s.ex // 2 - step, 2 + (step == 1), two_layers, start)
+            return tuple(ghosts), tuple(packed)
+
+        zeros = tuple(jnp.zeros((24, z), F32) for _ in range(q)) if step == 0 else ()
+        ghosts = tuple(
+            pltpu.roll(flat_beyond[(step * q + f) * 24 + skip : (step * q + f) * 24 + skip + height, :], z - 6 * step - 3, 1)
+            for f in range(q)
+        )
+        _, packed = unrolled(0, s.ex // 2 - step, 2 + (step == 1), two_layers, (ghosts, zeros))
         if step == 2:
             break
         for f in range(q):
             if step == 0:
-                nearest[1, f] = packed[f]
+                nearest[1, f] = pltpu.roll(packed[f], (6 * s.ex + 3) % z, 1)
             ghost, near = beyond[step, f], nearest[step, f]
             value = advanced(
                 None if step == 0 else beyond[0, f],
@@ -403,7 +406,7 @@
 
 
 def fine_kernel(s, f0, fw, flo_there, fhi_there, slab, out, avg, *scratch):
-    s1, s2, faces, ghost_rows, zface, flo, fhi, sems = scratch
+    s1, s2, faces, ghost_rows, zface, flo, fhi, summed, sems = scratch
     arrivals = [
         pltpu.make_async_copy(flo_there, flo, sems.at[4]),
         pltpu.make_async_copy(fhi_there, fhi, sems.at[5]),
@@ -461,7 +464,11 @@
     is_low, is_high = row_in == 0, row_in == y - 1
     flat_f0 = f0.reshape(q * fx * y, z)
 
-    def pair_of_layers(k, t, inner):
+    def ghosts_at(k, t):
+        shift = -(2 * s.ex * k + 2 * t) % z
+        return tuple(pltpu.roll(zface[i * y : (i + 1) * y, :], shift, 1) if shift else zface[i * y : (i + 1) * y, :] for i in range(2 * q))
+
+    def pair_of_layers(k, t, ghosts, inner):
         src, fraction = states[k], section_weights[k]
 
         def field(f, at):
@@ -495,8 +502,7 @@
                     flat = src.reshape(q * layers * PAD, z)
                     row = (f * layers + b + 1) * PAD + TOP
                     y_low, y_high = flat[pl.ds(row - 1, y), :], flat[pl.ds(row + 1, y), :]
-                ghost = zface[(odd * q + f) * y : (odd * q + f + 1) * y, :]
-                ghost = pltpu.roll(ghost, (2 * z - 2 * s.ex * k - 2 * t) if inner else -(2 * s.ex * k + 2 * t) % z, 1)
+                ghost = ghosts[odd * q + f]
                 value = advanced(
                     None if k == 0 else field(f, b - 2),
                     fraction,
@@ -512,6 +518,7 @@
                 made.append((f, b, value))
         for f, b, value in made:
             states[k + 1][f, b + 1, rows, :] = value
+        return tuple(pltpu.roll(g, z - 2, 1) for g in ghosts)
 
     for move in arrivals:
         move.wait()
@@ -520,30 +527,28 @@
         if k < 2:
             outer = 2 - k
             for t in list(range(outer)) + list(range(half - outer, half)):
-                pair_of_layers(k, t, False)
-            unrolled(outer, half - outer, 2, lambda t, g, k=k: pair_of_layers(k, t, True))
+                pair_of_layers(k, t, ghosts_at(k, t), False)
+            unrolled(outer, half - outer, 2, lambda t, g, k=k: pair_of_layers(k, t, g, True), ghosts_at(k, outer))
             continue
-        part = (half - 2) // 4
+        carried, part = ghosts_at(k, 1), (half - 2) // 4
         for i in range(4):
-            unrolled(1 + i * part, 1 + (i + 1) * part, 2, lambda t, g, k=k: pair_of_layers(k, t, True))
+            begin = 1 + i * part
+            carried = unrolled(begin, begin + part, 2, lambda t, g, k=k: pair_of_layers(k, t, g, True), carried)
             begin, end = 2 * part * i, 2 * part * (i + 1)
             moves.append(pltpu.make_async_copy(s1.at[:, 3 + begin : 3 + end, rows], out.at[:, begin:end], sems.at[i]))
             moves[-1].start()
     rz = lax.broadcasted_iota(jnp.int32, (z, z), 0)
     cz = lax.broadcasted_iota(jnp.int32, (z, z), 1)
-    flat = s1.reshape(q * layers * PAD, z)
+    flat = summed.reshape(q * s.x * y, z)
     pairs_z = [jnp.where(cz == rz // 2 + odd * s.sz, 0.125, 0.0).astype(BF16) for odd in range(2)]
+    for f in range(q):
+        for p in range(s.x):
+            both = s1[f, 3 + 2 * p, rows, :] + s1[f, 4 + 2 * p, rows, :]
+            summed[f, p] = both + pltpu.roll(both, y - 1, 0)
     for f in range(q):
         sums = []
         for odd in range(2):
-            parts = []
-            for p in range(s.x // 2):
-                base = (f * layers + 3 + 4 * p + 2 * odd) * PAD + TOP
-                part = None
-                for more in (0, 1, PAD, PAD + 1):
-                    piece = flat[pl.ds(base + more, y // 2, stride=2), :]
-                    part = piece if part is None else part + piece
-                parts.append(part)
+            parts = [flat[pl.ds((f * s.x + 2 * p + odd) * y, y // 2, stride=2), :] for p in range(s.x // 2)]
             sums.append(times(jnp.concatenate(parts, axis=0), pairs_z[odd]))
         avg[f] = (sums[0] + sums[1]).reshape(s.x // 2, y // 2, z)
     for move in moves:
@@ -676,6 +681,7 @@
             pltpu.VMEM((2 * q * y, z), F32),
             pltpu.VMEM(flo.shape, F32),
             pltpu.VMEM(fhi.shape, F32),
+            pltpu.VMEM((q, s.x, y, z), F32),
             pltpu.SemaphoreType.DMA((6,)),
         ],
         9,

time: 46.4 us -> 44.2 us (0.953)
  the two profiles are of different devices: /device:TPU:0 before, /device:TPU:2 now
where the time goes in v4:
time: 44.2 us; the launch traced here: 43.7 us
  Pallas kernels  22.5 us (51%)
  starting transfers between devices  11.8 us (27%)
  waiting for transfers between devices  7.04 us (16%)
  between operations  1.43 us (3%)
  local copies, waits for them, and re-layouts  0.71 us (2%)
    pallas_call x9, Pallas kernels, run(): pl.pallas_call(kernel, out_shape=tuple((space(dims, F32) for dims, space...  22.5 us
    ppermute x8, starting transfers between devices, ring(): lax.ppermute(array, axis, [(i, (i + by) % size) for i in range(size)])  10.5 us
    ppermute x8, waiting for transfers between devices, ring(): lax.ppermute(array, axis, [(i, (i + by) % size) for i in range(size)])  7.03 us
    ppermute x1, starting transfers between devices, z_columns(): return lax.ppermute(zown, 'gz', [(0, 1), (1, 0)])  1.33 us
  transfers between devices with their start and end apart: 9, of which 1 were waited for; matrix products, arithmetic and copies ran while one was open for 0% of the time, Pallas kernels for 46%

profile of v4, /device:TPU:2, one launch (start us, length us, event | category | flops | bytes accessed | tf_op | source)
XLA Modules:
  0.0 43.7 jit_solution(2037588553349741625)
XLA Ops:
  0.6 1.0 %pack_coarse.1 = (f32[18,16,128]{2,1,0:T(8,128)S(1)}, f32[18,16,128]{2,1,0:T(8,128)S(1)}) custom-call(f32[4,16,16,128]{3,2,1,0:T(8,128)} %c0.4, f32[3,16,16,128]{3,2,1,0:T(8,128)} %cw.7), custom_call_target="tpu_custom_call" | custom-call | flops 1 | bytes 1 | tf_op jit(solution)/shard_map/pack_coarse/pallas_call | solution.py:583
  1.6 1.6 %collective-permute-start.6 = (f32[18,16,128]{2,1,0:T(8,128)S(1)}, f32[18,16,128]{2,1,0:T(8,128)S(1)}, u32[]{:S(2)}, u32[]{:S(2)}) collective-permute-start(f32[18,16,128]{2,1,0:T(8,128)S(1)} %get-tuple-element.160), channel_id=1, source_target_pairs={{0,8},{8,16},{16,24},{24,0},{1,9},{9,17},{17,25},{25,1},{2,10},{10... | collective-permute-start | bytes 442376 | tf_op jit(solution)/shard_map/ppermute | solution.py:597
  3.2 0.0 copy-start
  3.3 0.0 copy-start.1
  3.3 2.2 %collective-permute-start.7 = (f32[18,16,128]{2,1,0:T(8,128)S(1)}, f32[18,16,128]{2,1,0:T(8,128)S(1)}, u32[]{:S(2)}, u32[]{:S(2)}) collective-permute-start(f32[18,16,128]{2,1,0:T(8,128)S(1)} %get-tuple-element.161), channel_id=1, source_target_pairs={{0,24},{8,0},{16,8},{24,16},{1,25},{9,1},{17,9},{25,17},{2,26},{10... | collective-permute-start | bytes 442376 | tf_op jit(solution)/shard_map/ppermute | solution.py:597
  5.5 1.6 %pack_fine.1 = (f32[20,16,128]{2,1,0:T(8,128)}, f32[20,16,128]{2,1,0:T(8,128)S(1)}) custom-call(f32[4,32,16,128]{3,2,1,0:T(8,128)} %f0.1, f32[3,32,16,128]{3,2,1,0:T(8,128)} %fw.1), custom_call_target="tpu_custom_call" | custom-call | flops 1 | bytes 1 | tf_op jit(solution)/shard_map/pack_fine/pallas_call | solution.py:583
  7.8 0.1 collective-permute-start.10
  7.9 3.8 %collective-permute-start.11 = (f32[20,16,128]{2,1,0:T(8,128)S(1)}, f32[20,16,128]{2,1,0:T(8,128)}, u32[]{:S(2)}, u32[]{:S(2)}) collective-permute-start(f32[20,16,128]{2,1,0:T(8,128)S(1)} %get-tuple-element.167), channel_id=1, source_target_pairs={{0,24},{8,0},{16,8},{24,16},{1,25},{9,1},{17,9},{25,17},{2,26},{10... | collective-permute-start | bytes 491528 | tf_op jit(solution)/shard_map/ppermute | solution.py:597
  11.7 0.0 copy-done
  11.7 0.0 copy-done.1
  11.7 2.5 %inner.1 = (f32[304,128]{1,0:T(8,128)S(1)}, f32[4,2,16,128]{3,2,1,0:T(8,128)S(1)}) custom-call(f32[4,16,16,128]{3,2,1,0:T(8,128)S(1)} %copy-done, f32[3,16,16,128]{3,2,1,0:T(8,128)S(1)} %copy-done.1), custom_call_target="tpu_custom_call" | custom-call | flops 1 | bytes 1 | tf_op jit(solution)/shard_map/inner/pallas_call | solution.py:583
  14.2 0.0 collective-permute-done.6.lo
  14.2 0.0 collective-permute-done.7.hi
  14.2 0.8 %ypack.1 = (f32[318,128]{1,0:T(8,128)}, f32[318,128]{1,0:T(8,128)}) custom-call(f32[4,16,16,128]{3,2,1,0:T(8,128)S(1)} %copy-done, f32[3,16,16,128]{3,2,1,0:T(8,128)S(1)} %copy-done.1, f32[18,16,128]{2,1,0:T(8,128)S(1)} %collective-permute-done.6.lo, f32[18,16,128]{2,1,0:T(8,128)S(1)} %collective-permute-done.7.hi), custom_call_target="tpu_custom_call" | custom-call | flops 1 | bytes 1 | tf_op jit(solution)/shard_map/ypack/pallas_call | solution.py:583
  15.0 0.0 collective-permute-start.8
  15.0 1.7 %collective-permute-start.9 = (f32[318,128]{1,0:T(8,128)}, f32[318,128]{1,0:T(8,128)S(1)}, u32[]{:S(2)}, u32[]{:S(2)}) collective-permute-start(f32[318,128]{1,0:T(8,128)} %get-tuple-element.163), channel_id=1, source_target_pairs={{0,6},{2,0},{4,2},{6,4},{1,7},{3,1},{5,3},{7,5},{8,14},{10,8},{12,... | collective-permute-start | bytes 488456 | tf_op jit(solution)/shard_map/ppermute | solution.py:597
  16.8 1.7 %slab.1 = f32[304,128]{1,0:T(8,128)S(1)} custom-call(f32[4,16,16,128]{3,2,1,0:T(8,128)S(1)} %copy-done, f32[3,16,16,128]{3,2,1,0:T(8,128)S(1)} %copy-done.1, f32[18,16,128]{2,1,0:T(8,128)S(1)} %collective-permute-done.6.lo, f32[18,16,128]{2,1,0:T(8,128)S(1)} %collective-permute-done.7.hi, f32[304,128]{1,0:T(8,128)S(1)} %get-tuple-element.164.part, ...), custom_call_target="tpu_custom_call" | custom-call | flops 1 | bytes 1 | tf_op jit(solution)/shard_map/slab/pallas_call | solution.py:583
  18.5 0.0 copy-start.3
  18.5 7.1 %conditional.2 = (f32[304,128]{1,0:T(8,128)S(1)}) conditional(s32[]{:T(128)} %clamp.7, f32[304,128]{1,0:T(8,128)S(1)} %slab.1, f32[304,128]{1,0:T(8,128)S(1)} %slab.1, f32[304,128]{1,0:T(8,128)S(1)} %slab.1, f32[304,128]{1,0:T(8,128)S(1)} %slab.1), branch_computations={%region_0.1_spmd, %region_1.2_spmd, %region_2.3_spmd, %region_3.4_... | conditional | bytes 933936 | solution.py:608
  18.5 0.1 collective-permute-start
  18.6 7.0 %collective-permute-done = f32[304,128]{1,0:T(8,128)S(1)} collective-permute-done((f32[304,128]{1,0:T(8,128)S(1)}, f32[304,128]{1,0:T(8,128)S(1)}, u32[]{:S(2)}, u32[]{:S(2)}) %collective-permute-start) | collective-permute-done | bytes 155680 | tf_op jit(solution)/shard_map/cond/branch_1_fun/ppermute | solution.py:597
  25.6 0.0 copy-start.4
  25.7 0.7 %copy-done.4 = f32[304,128]{1,0:T(8,128)} copy-done((f32[304,128]{1,0:T(8,128)}, f32[304,128]{1,0:T(8,128)S(1)}, u32[]{:S(2)}) %copy-start.4) | copy-done | bytes 155672
  26.3 0.0 copy-start.2
  26.3 0.0 copy-start.5
  26.3 0.0 collective-permute-done.10.flo_there
  26.3 0.0 collective-permute-done.11.fhi_there
  26.3 0.0 collective-permute-done.8.below
  26.3 0.0 collective-permute-done.9.above
  26.4 0.5 %zpack.1 = f32[7,24,128]{2,1,0:T(8,128)S(1)} custom-call(f32[4,16,16,128]{3,2,1,0:T(8,128)S(1)} %copy-done, f32[3,16,16,128]{3,2,1,0:T(8,128)S(1)} %copy-done.1, f32[18,16,128]{2,1,0:T(8,128)S(1)} %collective-permute-done.6.lo, f32[18,16,128]{2,1,0:T(8,128)S(1)} %collective-permute-done.7.hi, f32[318,128]{1,0:T(8,128)S(1)} %collective-permute-done.8.below, ...), custom_call_target="tpu_custom_call" | custom-call | flops 1 | bytes 1 | tf_op jit(solution)/shard_map/zpack/pallas_call | solution.py:583
  26.9 1.3 %collective-permute-start.12 = (f32[7,24,128]{2,1,0:T(8,128)S(1)}, f32[7,24,128]{2,1,0:T(8,128)S(1)}, u32[]{:S(2)}, u32[]{:S(2)}) collective-permute-start(f32[7,24,128]{2,1,0:T(8,128)S(1)} %zpack.1), channel_id=1, source_target_pairs={{0,1},{1,0},{2,3},{3,2},{4,5},{5,4},{6,7},{7,6},{8,9},{9,8},{10,11... | collective-permute-start | bytes 258056 | tf_op jit(solution)/shard_map/ppermute | solution.py:619
  28.2 0.1 add_convert_fusion
  28.3 0.0 copy-done.3
  28.3 0.0 copy-done.2
  28.3 0.0 copy-done.5
  28.3 7.6 %fine.1 = (f32[4,32,16,128]{3,2,1,0:T(8,128)}, f32[4,8,8,128]{3,2,1,0:T(8,128)S(1)}) custom-call(f32[4,32,16,128]{3,2,1,0:T(8,128)S(1)} %copy-done.2, f32[3,32,16,128]{3,2,1,0:T(8,128)S(1)} %copy-done.3, f32[20,16,128]{2,1,0:T(8,128)} %collective-permute-done.10.flo_there, f32[20,16,128]{2,1,0:T(8,128)} %collective-permute-done.11.fhi_there, ...), custom_call_target="tpu_custom_call" | custom-call | flops 1 | bytes 1 | tf_op jit(solution)/shard_map/fine/pallas_call | solution.py:583
  35.9 0.0 collective-permute-done.12
  35.9 6.8 %conditional.3 = (f32[4,8,8,128]{3,2,1,0:T(8,128)S(1)}, f32[4,16,16,128]{3,2,1,0:T(8,128)S(1)}) conditional(s32[]{:T(128)} %clamp.6, (s32[1,2]{1,0:T(1,128)S(1)}, f32[4,16,16,128]{3,2,1,0:T(8,128)S(1)}, f32[3,16,16,128]{3,2,1,0:T(8,128)S(1)}, f32[18,16,128]{2,1,0:T(8,128)S(1)}, f32[18,16,128]{2,1,0:T(8,128)S(1)}, ...), branch_computations={%region_4.5_spmd, %region_5.6_spmd, %region_6.7_spmd, %region_7.8_... | conditional | flops 40000000 | bytes 4786488 | solution.py:608
  35.9 1.0 %collective-permute-start.5 = (f32[4,8,8,128]{3,2,1,0:T(8,128)S(1)}, f32[4,8,8,128]{3,2,1,0:T(8,128)S(1)}, u32[]{:S(2)}, u32[]{:S(2)}) collective-permute-start(f32[4,8,8,128]{3,2,1,0:T(8,128)S(1)} %get-tuple-element.119), channel_id=1, source_target_pairs={{0,24},{8,0},{16,8},{24,16},{1,25},{9,1},{17,9},{25,17},{2,26},{10... | collective-permute-start | bytes 393224 | tf_op jit(solution)/shard_map/cond/branch_3_fun/ppermute | solution.py:597
  36.9 5.8 %coarse.7 = f32[4,16,16,128]{3,2,1,0:T(8,128)S(1)} custom-call(s32[1,2]{1,0:T(1,128)S(1)} %get-tuple-element.120.sides, f32[4,16,16,128]{3,2,1,0:T(8,128)S(1)} %get-tuple-element.121.c0, f32[3,16,16,128]{3,2,1,0:T(8,128)S(1)} %get-tuple-element.122.cw, f32[18,16,128]{2,1,0:T(8,128)S(1)} %get-tuple-element.123.lo, f32[18,16,128]{2,1,0:T(8,128)S(1)} %get-tuple-element.124.hi, ...), custom_call_target="tpu_custom_call" | custom-call | flops 40000000 | bytes 4000000 | tf_op jit(solution)/shard_map/cond/branch_3_fun/coarse/pallas_call | solution.py:583
  42.7 0.0 collective-permute-done.5
  42.8 0.9 %merge.1 = f32[4,16,16,128]{3,2,1,0:T(8,128)} custom-call(f32[4,16,16,128]{3,2,1,0:T(8,128)S(1)} %get-tuple-element.174.c3, f32[4,8,8,128]{3,2,1,0:T(8,128)S(1)} %get-tuple-element.175.avg), custom_call_target="tpu_custom_call" | custom-call | flops 1 | bytes 1 | tf_op jit(solution)/shard_map/merge/pallas_call | solution.py:583
  (2 shorter events, 0.0 us)
Async XLA Ops:
  1.6 12.6 %collective-permute-start.6 = (f32[18,16,128]{2,1,0:T(8,128)S(1)}, f32[18,16,128]{2,1,0:T(8,128)S(1)}, u32[]{:S(2)}, u32[]{:S(2)}) collective-permute-start(f32[18,16,128]{2,1,0:T(8,128)S(1)} %get-tuple-element.160), channel_id=1, source_target_pairs={{0,8},{8,16},{16,24},{24,0},{1,9},{9,17},{17,25},{25,1},{2,10},{10... | collective-permute-start | bytes 442376 | tf_op jit(solution)/shard_map/ppermute | solution.py:597
  3.2 8.4 %copy-start = (f32[4,16,16,128]{3,2,1,0:T(8,128)S(1)}, f32[4,16,16,128]{3,2,1,0:T(8,128)}, u32[]{:S(2)}) copy-start(f32[4,16,16,128]{3,2,1,0:T(8,128)} %c0.4) | copy-start | bytes 1572868
  3.3 8.4 %copy-start.1 = (f32[3,16,16,128]{3,2,1,0:T(8,128)S(1)}, f32[3,16,16,128]{3,2,1,0:T(8,128)}, u32[]{:S(2)}) copy-start(f32[3,16,16,128]{3,2,1,0:T(8,128)} %cw.7) | copy-start | bytes 1179652
  3.3 10.9 %collective-permute-start.7 = (f32[18,16,128]{2,1,0:T(8,128)S(1)}, f32[18,16,128]{2,1,0:T(8,128)S(1)}, u32[]{:S(2)}, u32[]{:S(2)}) collective-permute-start(f32[18,16,128]{2,1,0:T(8,128)S(1)} %get-tuple-element.161), channel_id=1, source_target_pairs={{0,24},{8,0},{16,8},{24,16},{1,25},{9,1},{17,9},{25,17},{2,26},{10... | collective-permute-start | bytes 442376 | tf_op jit(solution)/shard_map/ppermute | solution.py:597
  7.8 18.5 %collective-permute-start.10 = (f32[20,16,128]{2,1,0:T(8,128)}, f32[20,16,128]{2,1,0:T(8,128)}, u32[]{:S(2)}, u32[]{:S(2)}) collective-permute-start(f32[20,16,128]{2,1,0:T(8,128)} %get-tuple-element.166), channel_id=1, source_target_pairs={{0,8},{8,16},{16,24},{24,0},{1,9},{9,17},{17,25},{25,1},{2,10},{10... | collective-permute-start | bytes 491528 | tf_op jit(solution)/shard_map/ppermute | solution.py:597
  7.9 18.4 %collective-permute-start.11 = (f32[20,16,128]{2,1,0:T(8,128)S(1)}, f32[20,16,128]{2,1,0:T(8,128)}, u32[]{:S(2)}, u32[]{:S(2)}) collective-permute-start(f32[20,16,128]{2,1,0:T(8,128)S(1)} %get-tuple-element.167), channel_id=1, source_target_pairs={{0,24},{8,0},{16,8},{24,16},{1,25},{9,1},{17,9},{25,17},{2,26},{10... | collective-permute-start | bytes 491528 | tf_op jit(solution)/shard_map/ppermute | solution.py:597
  15.0 11.3 %collective-permute-start.8 = (f32[318,128]{1,0:T(8,128)}, f32[318,128]{1,0:T(8,128)S(1)}, u32[]{:S(2)}, u32[]{:S(2)}) collective-permute-start(f32[318,128]{1,0:T(8,128)} %get-tuple-element.162), channel_id=1, source_target_pairs={{0,2},{2,4},{4,6},{6,0},{1,3},{3,5},{5,7},{7,1},{8,10},{10,12},{12... | collective-permute-start | bytes 488456 | tf_op jit(solution)/shard_map/ppermute | solution.py:597
  15.0 11.3 %collective-permute-start.9 = (f32[318,128]{1,0:T(8,128)}, f32[318,128]{1,0:T(8,128)S(1)}, u32[]{:S(2)}, u32[]{:S(2)}) collective-permute-start(f32[318,128]{1,0:T(8,128)} %get-tuple-element.163), channel_id=1, source_target_pairs={{0,6},{2,0},{4,2},{6,4},{1,7},{3,1},{5,3},{7,5},{8,14},{10,8},{12,... | collective-permute-start | bytes 488456 | tf_op jit(solution)/shard_map/ppermute | solution.py:597
  18.5 9.8 %copy-start.3 = (f32[3,32,16,128]{3,2,1,0:T(8,128)S(1)}, f32[3,32,16,128]{3,2,1,0:T(8,128)}, u32[]{:S(2)}) copy-start(f32[3,32,16,128]{3,2,1,0:T(8,128)} %fw.1) | copy-start | bytes 2359300
  18.5 7.1 %collective-permute-start = (f32[304,128]{1,0:T(8,128)S(1)}, f32[304,128]{1,0:T(8,128)S(1)}, u32[]{:S(2)}, u32[]{:S(2)}) collective-permute-start(f32[304,128]{1,0:T(8,128)S(1)} %param.1), channel_id=1, source_target_pairs={{0,8},{8,16},{16,24},{24,0},{1,9},{9,17},{17,25},{25,1},{2,10},{10... | collective-permute-start | bytes 466952 | tf_op jit(solution)/shard_map/cond/branch_1_fun/ppermute | solution.py:597
  25.6 0.7 %copy-start.4 = (f32[304,128]{1,0:T(8,128)}, f32[304,128]{1,0:T(8,128)S(1)}, u32[]{:S(2)}) copy-start(f32[304,128]{1,0:T(8,128)S(1)} %get-tuple-element.185.slab) | copy-start | bytes 466948
  26.3 2.0 %copy-start.2 = (f32[4,32,16,128]{3,2,1,0:T(8,128)S(1)}, f32[4,32,16,128]{3,2,1,0:T(8,128)}, u32[]{:S(2)}) copy-start(f32[4,32,16,128]{3,2,1,0:T(8,128)} %f0.1) | copy-start | bytes 3145732
  26.3 2.0 %copy-start.5 = (f32[304,128]{1,0:T(8,128)S(1)}, f32[304,128]{1,0:T(8,128)}, u32[]{:S(2)}) copy-start(f32[304,128]{1,0:T(8,128)} %copy-done.4) | copy-start | bytes 466948
  26.9 9.0 %collective-permute-start.12 = (f32[7,24,128]{2,1,0:T(8,128)S(1)}, f32[7,24,128]{2,1,0:T(8,128)S(1)}, u32[]{:S(2)}, u32[]{:S(2)}) collective-permute-start(f32[7,24,128]{2,1,0:T(8,128)S(1)} %zpack.1), channel_id=1, source_target_pairs={{0,1},{1,0},{2,3},{3,2},{4,5},{5,4},{6,7},{7,6},{8,9},{9,8},{10,11... | collective-permute-start | bytes 258056 | tf_op jit(solution)/shard_map/ppermute | solution.py:619
  35.9 6.8 %collective-permute-start.5 = (f32[4,8,8,128]{3,2,1,0:T(8,128)S(1)}, f32[4,8,8,128]{3,2,1,0:T(8,128)S(1)}, u32[]{:S(2)}, u32[]{:S(2)}) collective-permute-start(f32[4,8,8,128]{3,2,1,0:T(8,128)S(1)} %get-tuple-element.119), channel_id=1, source_target_pairs={{0,24},{8,0},{16,8},{24,16},{1,25},{9,1},{17,9},{25,17},{2,26},{10... | collective-permute-start | bytes 393224 | tf_op jit(solution)/shard_map/cond/branch_3_fun/ppermute | solution.py:597
